TPU v7x, 512 devices: a whole 4x4x16 slice. The times are simulated.
512 devices in a mesh: row: 16 (over z), col: 32 (over x, y, core).
Axes of the slice: x: 4, y: 4, z: 16, core: 2. Of those that a mesh axis runs over, the one named last changes fastest.
Arguments:
- left_factors: bfloat16 [96, 96, 96, 512], P('row', 'col'), may hold values from -6 to 6
- right_factors: bfloat16 [96, 96, 96, 512], P('row', 'col'), may hold values from -0.015625 to 0.015625
- ranks: int32 [96, 96], P('row', 'col'), may hold values from 16 to 96
- sketch_left: bfloat16 [96, 128, 512], P('row'), may hold values from -32 to 32
- sketch_right: bfloat16 [512, 128], replicated, may hold values from -32 to 32
- upper_inverse: bfloat16 [512, 512], replicated, as said below
- step: int32 [1], replicated, may hold values from 48 to 94
Outputs:
- range_sketch: bfloat16 [96, 128, 512], P('row')
- factored_sketch: bfloat16 [96, 128, 512], P('row')
Inputs may be any that keep to these rules, and one draw needn't show every extreme that they name: `ranks`: rows of a tile's factors at or beyond its rank are not part of the tile. `step`: columns before this one are factored. `upper_inverse`: upper triangular.
All inputs are finite; a program needn't handle non-finite values.
Results may differ from a plain program's by a relative error of at most 0.0071.
Values may be sent and summed in bfloat16 or wider, within the bound.
A program may use at most 64 MiB of HBM per device.

v0:
```python
import jax
import jax.numpy as jnp
from jax import lax
from jax.sharding import PartitionSpec as P


def from_root(block, axis, source):
    block = jnp.where(lax.axis_index(axis) == source, block, jnp.zeros_like(block))
    return lax.psum(block, axis)


def share_terms(
    panel_left, panel_right, sketch_left, sketch_right, row_ids, column, share_rows, share_start
):
    sketch_cols = sketch_left.shape[1]
    tile_size = sketch_left.shape[2]
    flat_ids = share_start + jnp.arange(share_rows, dtype=jnp.int32)
    which_row = flat_ids // sketch_cols
    which_probe = flat_ids % sketch_cols
    rows_left = jnp.take(panel_left, which_row, axis=0)
    rows_right = jnp.take(panel_right, which_row, axis=0)
    probe_cols = jnp.take(sketch_right, which_probe, axis=1)
    flat_sketch = lax.dynamic_slice_in_dim(
        sketch_left.reshape(-1, tile_size), share_start, share_rows, 0
    )
    own_reduced = jnp.einsum(
        "qrt,tq->qr", rows_right, probe_cols, preferred_element_type=jnp.float32
    ).astype(jnp.bfloat16)
    own_range = jnp.einsum("qr,qrt->qt", own_reduced, rows_left, preferred_element_type=jnp.float32)
    own_probe = jnp.einsum(
        "qt,qrt->qr", flat_sketch, rows_left, preferred_element_type=jnp.float32
    ).astype(jnp.bfloat16)
    own_co = jnp.einsum("qr,qrt->qt", own_probe, rows_right, preferred_element_type=jnp.float32)
    row_weight = (jnp.take(row_ids, which_row) > column).astype(jnp.float32)
    return (row_weight[:, None] * own_range, row_weight[:, None] * own_co)


def body(left_factors, right_factors, ranks, sketch_left, sketch_right, upper_inverse, step):
    tile_rows, tile_cols, rank_max, tile_size = left_factors.shape
    sketch_cols = sketch_left.shape[1]
    column = step[0]
    row_first = lax.axis_index("row") * tile_rows
    col_first = lax.axis_index("col") * tile_cols
    levels = jnp.arange(rank_max, dtype=jnp.int32)
    rank_keep = levels[None, None, :] < ranks[:, :, None]
    masked = jnp.where(rank_keep[..., None], left_factors, jnp.zeros_like(left_factors))
    slot_index = column % tile_cols
    owner_col = column // tile_cols
    own_left = lax.dynamic_index_in_dim(masked, slot_index, 1, keepdims=False)
    own_right = lax.dynamic_index_in_dim(right_factors, slot_index, 1, keepdims=False)
    panel_left, panel_right = (
        from_root(own_left, "col", owner_col),
        from_root(own_right, "col", owner_col),
    )
    source_row = col_first // tile_rows
    offset = col_first - source_row * tile_rows
    to_send = (panel_left, panel_right)
    got_left, got_right = (
        from_root(to_send[0], "row", source_row),
        from_root(to_send[1], "row", source_row),
    )
    upper_left = lax.dynamic_slice_in_dim(got_left, offset, tile_cols, 0)
    upper_right = lax.dynamic_slice_in_dim(got_right, offset, tile_cols, 0)
    row_ids = row_first + jnp.arange(tile_rows, dtype=jnp.int32)
    col_ids = col_first + jnp.arange(tile_cols, dtype=jnp.int32)
    active = (row_ids[:, None] > column) & (col_ids[None, :] < column)
    coupling = jnp.einsum(
        "ijrt,jst->ijrs", right_factors, upper_left, preferred_element_type=jnp.float32
    ).astype(jnp.bfloat16)
    reduced = jnp.einsum(
        "jrt,tp->jrp", upper_right, sketch_right, preferred_element_type=jnp.float32
    ).astype(jnp.bfloat16)
    mixed = jnp.einsum("ijrs,jsp->ijrp", coupling, reduced, preferred_element_type=jnp.float32)
    mixed = jnp.where(active[:, :, None, None], mixed, jnp.float32(0.0)).astype(jnp.bfloat16)
    range_terms = jnp.einsum("ijrp,ijrt->ipt", mixed, masked, preferred_element_type=jnp.float32)
    probe_left = jnp.einsum(
        "ipt,ijrt->ijpr", sketch_left, masked, preferred_element_type=jnp.float32
    ).astype(jnp.bfloat16)
    folded = jnp.einsum("ijpr,ijrs->ijps", probe_left, coupling, preferred_element_type=jnp.float32)
    folded = jnp.where(active[:, :, None, None], folded, jnp.float32(0.0)).astype(jnp.bfloat16)
    co_terms = jnp.einsum("ijps,jst->ipt", folded, upper_right, preferred_element_type=jnp.float32)
    flat_range = (-range_terms).reshape(tile_rows * sketch_cols, tile_size)
    flat_co = (-co_terms).reshape(tile_rows * sketch_cols, tile_size)
    share_rows = tile_rows * sketch_cols // lax.axis_size("col")
    share_start = lax.axis_index("col") * share_rows
    own_range, own_co = share_terms(
        panel_left, panel_right, sketch_left, sketch_right, row_ids, column, share_rows, share_start
    )
    range_part = lax.dynamic_update_slice_in_dim(
        flat_range,
        lax.dynamic_slice_in_dim(flat_range, share_start, share_rows, 0) + own_range,
        share_start,
        0,
    )
    co_part = lax.dynamic_update_slice_in_dim(
        flat_co,
        lax.dynamic_slice_in_dim(flat_co, share_start, share_rows, 0) + own_co,
        share_start,
        0,
    )
    totals = lax.psum((range_part, co_part), "col")
    range_sketch = totals[0].astype(jnp.bfloat16).reshape(tile_rows, sketch_cols, tile_size)
    factored = (
        jnp.dot(totals[1].astype(jnp.bfloat16), upper_inverse, preferred_element_type=jnp.float32)
        .astype(jnp.bfloat16)
        .reshape(tile_rows, sketch_cols, tile_size)
    )
    return (range_sketch, factored)


def solution(mesh):
    return jax.shard_map(
        body,
        mesh=mesh,
        in_specs=(
            P("row", "col", None, None),
            P("row", "col", None, None),
            P("row", "col"),
            P("row", None, None),
            P(),
            P(),
            P(),
        ),
        out_specs=(P("row", None, None), P("row", None, None)),
        check_vma=False,
    )
```

profile of v0, /device:TPU:32, one launch (start us, length us, event | category | flops | bytes accessed | tf_op | source)
XLA Modules:
  0.0 465.8 jit_solution(93375095914885833)
XLA Ops:
  7.2 0.0 copy-start
  7.2 0.0 all-reduce.7.cloned.1.call-start
  8.0 0.8 iota_compare_fusion
  8.7 1.6 copy_select_fusion
  10.4 0.0 copy-start.6
  10.4 2.4 select_bitcast_fusion
  12.7 0.0 all-reduce.7.cloned.1.call-update
  12.8 0.0 all-reduce.9.cloned.1.call-start
  13.0 0.7 gather_fusion
  13.7 0.0 copy-done.6
  13.8 0.1 copy.18
  13.9 0.6 gather_fusion.1
  14.5 0.0 copy-done
  14.5 0.1 broadcast_and_fusion
  14.6 0.1 select_bitcast_fusion.2
  14.7 138.1 %all-reduce.7.cloned.1.call-done = (bf16[6,96,512]{2,1,0:T(8,128)(2,1)}, bf16[6,96,512]{2,1,0:T(8,128)(2,1)}) async-done(((bf16[6,96,512]{2,1,0:T(8,128)(2,1)}, bf16[6,96,512]{2,1,0:T(8,128)(2,1)}), (bf16[6,96,512]{2,1,0:T(8,128)(2,1)}, bf16[6,96,512]{2,1,0:T(8,128)(2,1)})) %all-reduce.7.cloned.1.call-update) | async-done | bytes 1179664 | tf_op jit(solution)/shard_map/psum | solution.py:9
  152.8 0.0 copy-start.2
  152.8 0.9 broadcast_select_fusion.7
  153.7 0.9 broadcast_select_fusion.6
  154.5 0.0 copy-done.2
  154.5 2.2 gather_fusion.3
  156.7 0.0 all-reduce.9.cloned.1.call-update
  156.7 0.0 copy-start.1
  156.8 2.5 fusion.18
  159.3 0.0 copy-done.1
  159.3 2.2 gather_fusion.2
  161.5 0.0 copy-start.4
  161.5 2.6 fusion.17
  164.1 0.0 copy-start.3
  164.1 0.0 copy-done.4
  164.1 0.5 fusion.16
  164.6 1.2 copy-done.3
  165.7 0.5 fusion.19
  166.2 130.7 %all-reduce.9.cloned.1.call-done = (bf16[6,96,512]{2,1,0:T(8,128)(2,1)}, bf16[6,96,512]{2,1,0:T(8,128)(2,1)}) async-done(((bf16[6,96,512]{2,1,0:T(8,128)(2,1)}, bf16[6,96,512]{2,1,0:T(8,128)(2,1)}), (bf16[6,96,512]{2,1,0:T(8,128)(2,1)}, bf16[6,96,512]{2,1,0:T(8,128)(2,1)})) %all-reduce.9.cloned.1.call-update) | async-done | bytes 1179664 | tf_op jit(solution)/shard_map/psum | solution.py:9
  296.9 0.0 copy-start.5
  296.9 3.2 fusion.12
  300.1 0.0 copy-done.5
  300.1 0.2 fusion.15
  300.3 2.5 fusion.11
  302.8 3.1 bitcast_negate_fusion.1
  305.9 1.6 bitcast_negate_fusion
  307.6 1.5 fusion.35
  309.0 147.4 %all-reduce.10 = (bf16[768,512]{1,0:T(8,128)(2,1)}, bf16[768,512]{1,0:T(8,128)(2,1)S(1)}) all-reduce(f32[768,512]{1,0:T(8,128)} %get-tuple-element.10, f32[768,512]{1,0:T(8,128)S(1)} %get-tuple-element.9), channel_id=1, replica_groups=mesh['row'=16,'col'=32] {'col'}, use_global_device_ids=true, to_apply=%region_4.6 | all-reduce | flops 786432 | bytes 4718592 | tf_op jit(solution)/shard_map/psum | solution.py:101
  456.5 2.5 convolution_convert_fusion
  (14 shorter events, 0.1 us)
Async XLA Ops:
  7.2 7.3 %copy-start = (bf16[6,128,512]{2,1,0:T(8,128)(2,1)S(1)}, bf16[6,128,512]{2,1,0:T(8,128)(2,1)}, u32[]{:S(2)}) copy-start(bf16[6,128,512]{2,1,0:T(8,128)(2,1)} %param.12) | copy-start | bytes 2359300
  7.2 145.6 %all-reduce.7.cloned.1.call-start = ((), (), s32[]{:S(2)}) async-start(), calls=%async_computation | async-start | bytes 2359296 | tf_op jit(solution)/shard_map/psum | solution.py:9
  10.4 3.4 copy-start.6
  12.8 284.1 %all-reduce.9.cloned.1.call-start = ((), (), s32[]{:S(2)}) async-start(), calls=%async_computation.1 | async-start | bytes 2359296 | tf_op jit(solution)/shard_map/psum | solution.py:9
  152.8 1.7 copy-start.2
  156.7 2.5 copy-start.1
  161.5 2.6 copy-start.4
  164.1 1.7 copy-start.3
  296.9 3.2 copy-start.5
Sparse Core Ops, SparseCore 0:
  12.9 139.8 all-reduce.6
  156.9 139.9 all-reduce.8
where the time goes:
time: 466 us
  waiting for transfers between devices  269 us (58%)
  blocking collectives  147 us (32%)
  matrix products  19.2 us (4%)
  between operations  15 us (3%)
  other arithmetic  8.25 us (2%)
  local copies, waits for them, and re-layouts  7.02 us (2%)
    psum x2, waiting for transfers between devices, from_root(): return lax.psum(block, axis)  269 us
    psum x1, blocking collectives, body(): totals = lax.psum((range_part, co_part), 'col')  147 us
  transfers between devices with their start and end apart: 2, of which 2 were waited for; matrix products, arithmetic and copies ran while one was open for 2% of the time, Pallas kernels for 0%

commit v1 on v0

v1 whole, which is shorter than its diff:
```python
import functools

import jax
import jax.numpy as jnp
from jax import lax
from jax.experimental import pallas as pl
from jax.experimental.pallas import tpu as pltpu
from jax.sharding import PartitionSpec as P

MESH = pl.DeviceIdType.MESH
F32 = jnp.float32
BF16 = jnp.bfloat16
FIRST = 8
LAST = 15
HALF = 48
CHUNKS = 12


def remote(src, dst, send_sem, recv_sem, device):
    return pltpu.make_async_remote_copy(
        src_ref=src,
        dst_ref=dst,
        send_sem=send_sem,
        recv_sem=recv_sem,
        device_id=device,
        device_id_type=MESH,
    )


def gather_kernel(ranks_ref, step_ref, left_ref, right_ref, panel_ref, sems):
    column = step_ref[0]
    slot = lax.rem(column, 3)

    @pl.when(lax.axis_index("col") == column // 3)
    def _():
        copies = [
            pltpu.make_async_copy(left_ref.at[:, slot], panel_ref.at[:, 0], sems.at[0]),
            pltpu.make_async_copy(right_ref.at[:, slot], panel_ref.at[:, 1], sems.at[1]),
        ]
        for copy in copies:
            copy.start()
        for copy in copies:
            copy.wait()
        level = lax.broadcasted_iota(jnp.int32, (96, 512), 0)
        for i in range(6):
            tile = panel_ref[i, 0]
            panel_ref[i, 0] = jnp.where(level < ranks_ref[slot, i], tile, jnp.zeros_like(tile))


def gather_panel(ranks, step, left, right):
    return pl.pallas_call(
        gather_kernel,
        out_shape=jax.ShapeDtypeStruct((6, 2, 96, 512), BF16),
        in_specs=[
            pl.BlockSpec(memory_space=pltpu.SMEM),
            pl.BlockSpec(memory_space=pltpu.SMEM),
            pl.BlockSpec(memory_space=pl.ANY),
            pl.BlockSpec(memory_space=pl.ANY),
        ],
        out_specs=pl.BlockSpec(memory_space=pltpu.VMEM),
        scratch_shapes=[pltpu.SemaphoreType.DMA((2,))],
        compiler_params=pltpu.CompilerParams(vmem_limit_bytes=62 * 2**20),
        name="gather_panel",
    )(ranks, step, left, right)


def panel_kernel(
    owner, panel_ref, out_ref, extra_ref, src_send, up_send, down_send, recv_sem,
    extra_up, extra_down, extra_recv, give_send, local_sem,
):
    z = lax.axis_index("row")
    c = lax.axis_index("col")
    s = c // 2
    kind = c % 2
    owner_line = owner // 2
    owner_core = owner % 2
    carrier = owner + 1 - 2 * owner_core
    low = s < FIRST
    high = jnp.logical_not(low)
    home = z == s
    is_owner = c == owner
    is_carrier = c == carrier
    target = z >= FIRST
    way = (c == 0) & (z == 4)
    up = (low & (kind == 0) & (home | way | (target & (z < LAST)))) | (high & (z >= s) & (z < LAST))
    down = (low & (kind == 1) & (home | (z > FIRST))) | (high & (z <= s) & (z > FIRST))
    up = up & jnp.logical_not(is_owner)
    down = down & jnp.logical_not(is_owner)
    up_to = jnp.where((c == 0) & (z == 0), 4, jnp.where(z < FIRST, FIRST, z + 1))
    down_to = jnp.where(z < FIRST, LAST, z - 1)
    from_owner = home & jnp.logical_not(is_owner)
    from_below = ((low & (kind == 0)) | (high & (z > s))) & target | way
    from_above = ((low & (kind == 1)) | (high & (z < s))) & target
    from_below = from_below & jnp.logical_not(is_owner)
    from_above = from_above & jnp.logical_not(is_owner)
    entry = jnp.where(c == 0, 4, s)
    below = jnp.where(way, 0, jnp.where(low & (z == FIRST), entry, z - 1))
    above = jnp.where(low & (z == LAST), s, z + 1)
    from_carrier = is_owner & target & (z != owner_line)
    receives = from_owner | from_below | from_above | from_carrier
    sends_home = is_owner & (z != owner_line)
    holds_own = is_owner & (z == owner_line)
    carries = is_carrier & target

    barrier = pltpu.get_barrier_semaphore()

    def greet(flag, device):
        @pl.when(flag)
        def _():
            pl.semaphore_signal(barrier, inc=1, device_id=device, device_id_type=MESH)

    greet(from_owner, (z, owner))
    greet(from_below, (below, c))
    greet(from_above, (above, c))
    greet(from_carrier, (z, carrier))

    def count(flag, amount=1):
        return jnp.where(flag, amount, 0)

    peers = (
        count(is_owner, jnp.where(z == owner_line, 1, 2))
        + count(up)
        + count(down)
        + count(carries & (z != owner_line))
    )

    @pl.when(peers > 0)
    def _():
        pl.semaphore_wait(barrier, peers)

    def piece(q):
        return q // 4, (q // 2) % 2, pl.ds(pl.multiple_of((q % 2) * HALF, HALF), HALF)

    def src_copy(core, q):
        t, side, rows = piece(q)
        return remote(
            panel_ref.at[3 * core + t, side, rows],
            out_ref.at[t, side, rows],
            src_send.at[core, q],
            recv_sem.at[q],
            (z, 2 * z + core),
        )

    def lend_copy(q):
        t, side, rows = piece(q)
        return remote(
            panel_ref.at[3 * owner_core + t, side, rows],
            extra_ref.at[t, side, rows],
            src_send.at[owner_core, q],
            extra_recv.at[q],
            (z, carrier),
        )

    def chain_copy(ref, send, recv, device, q):
        t, side, rows = piece(q)
        here = ref.at[t, side, rows]
        return remote(here, here, send.at[q], recv.at[q], device)

    def give_copy(q):
        t, side, rows = piece(q)
        return remote(
            extra_ref.at[t, side, rows], out_ref.at[t, side, rows], give_send.at[q], recv_sem.at[q], (z, owner)
        )

    def up_copy(q):
        return chain_copy(out_ref, up_send, recv_sem, (up_to, c), q)

    def down_copy(q):
        return chain_copy(out_ref, down_send, recv_sem, (down_to, c), q)

    def extra_up_copy(q):
        return chain_copy(extra_ref, extra_up, extra_recv, (z + 1, c), q)

    def extra_down_copy(q):
        return chain_copy(extra_ref, extra_down, extra_recv, (z - 1, c), q)

    def loop(flag, body):
        @pl.when(flag)
        def _():
            lax.fori_loop(0, CHUNKS, lambda q, _: (body(q), 0)[1], 0)

    def when(flag, body):
        @pl.when(flag)
        def _():
            body()

    loop(holds_own, lambda q: lend_copy(q).start())
    for core in range(2):
        flag = is_owner if core != owner_core else sends_home
        loop(flag, lambda q, core=core: src_copy(core, q).start())

    @pl.when(holds_own)
    def _():
        copy = pltpu.make_async_copy(panel_ref.at[pl.ds(3 * owner_core, 3)], out_ref, local_sem)
        copy.start()
        copy.wait()

    def relay(q):
        when(receives, lambda: chain_copy(out_ref, up_send, recv_sem, (z, c + 1 - 2 * kind), q).wait_recv())
        when(up, lambda: up_copy(q).start())
        when(down, lambda: down_copy(q).start())

        @pl.when(carries)
        def _():
            chain_copy(extra_ref, extra_up, extra_recv, (z, owner), q).wait_recv()
            when((z >= owner_line) & (z < LAST), lambda: extra_up_copy(q).start())
            when((z <= owner_line) & (z > FIRST), lambda: extra_down_copy(q).start())
            when(z != owner_line, lambda: give_copy(q).start())

    lax.fori_loop(0, CHUNKS, lambda q, _: (relay(q), 0)[1], 0)

    loop(holds_own, lambda q: lend_copy(q).wait_send())
    for core in range(2):
        flag = is_owner if core != owner_core else sends_home
        loop(flag, lambda q, core=core: src_copy(core, q).wait_send())
    loop(up, lambda q: up_copy(q).wait_send())
    loop(down, lambda q: down_copy(q).wait_send())
    loop(carries & (z >= owner_line) & (z < LAST), lambda q: extra_up_copy(q).wait_send())
    loop(carries & (z <= owner_line) & (z > FIRST), lambda q: extra_down_copy(q).wait_send())
    loop(carries & (z != owner_line), lambda q: give_copy(q).wait_send())


def spread_panel(owner, panel):
    return pl.pallas_call(
        functools.partial(panel_kernel, owner),
        out_shape=jax.ShapeDtypeStruct((3, 2, 96, 512), BF16),
        in_specs=[pl.BlockSpec(memory_space=pltpu.VMEM)],
        out_specs=pl.BlockSpec(memory_space=pltpu.VMEM),
        scratch_shapes=[
            pltpu.VMEM((3, 2, 96, 512), BF16),
            pltpu.SemaphoreType.DMA((2, CHUNKS)),
            pltpu.SemaphoreType.DMA((CHUNKS,)),
            pltpu.SemaphoreType.DMA((CHUNKS,)),
            pltpu.SemaphoreType.DMA((CHUNKS,)),
            pltpu.SemaphoreType.DMA((CHUNKS,)),
            pltpu.SemaphoreType.DMA((CHUNKS,)),
            pltpu.SemaphoreType.DMA((CHUNKS,)),
            pltpu.SemaphoreType.DMA((CHUNKS,)),
            pltpu.SemaphoreType.DMA,
        ],
        compiler_params=pltpu.CompilerParams(
            collective_id=owner - 15, has_side_effects=True, vmem_limit_bytes=16 * 2**20
        ),
        name="spread_panel",
    )(panel)


def dot_nt(a, b):
    return lax.dot_general(a, b, (((1,), (1,)), ((), ())), preferred_element_type=F32)


def dot_nn(a, b):
    return jnp.dot(a, b, preferred_element_type=F32)


def row_kernel(
    ranks_ref, step_ref, left_hbm, right_hbm, probe_hbm, upper_ref, sketch_ref, solve_ref, out_ref,
    left_ref, right_ref, probe_ref, stack_ref, reduced_ref,
    send_ref, got_ref, acc_ref, cur_ref, a1_ref, a2_ref, b_ref, blk_ref,
    load_sem, send_sem, recv_sem, b_send, b_recv, pair_send, pair_recv,
):
    z = lax.axis_index("row")
    c = lax.axis_index("col")
    x = c // 8
    y = (c // 2) % 4
    core = c % 2
    sibling = (z, c + 1 - 2 * core)
    place = (x, y)
    order = (0, 3, 1, 4, 2, 5)

    def near(axis, by):
        if axis == 0:
            return (z, ((x + by + 4) % 4) * 8 + y * 2 + core)
        return (z, x * 8 + ((y + by + 4) % 4) * 2 + core)

    def rows32(b):
        return pl.ds(pl.multiple_of(((b + 4) % 4) * 32, 32), 32)

    def rows16(b, h):
        return pl.ds(pl.multiple_of(((b + 4) % 4) * 32 + 16 * h, 16), 16)

    def cols(b):
        return pl.ds(pl.multiple_of(((b + 4) % 4) * 128, 128), 128)

    def axes(a):
        return (0, 1) if a < 3 else (1, 0)

    def two_ways(a, n, src, dst):
        axis = axes(a)[0]
        return [
            remote(src(d), dst(d), send_sem.at[a, n, d], recv_sem.at[a, n, d], near(axis, 1 - 2 * d))
            for d in range(2)
        ]

    def copies(a, n):
        first, second = axes(a)
        u, v = place[first], place[second]
        mine = out_ref.at[core, a]
        if n == 0:
            return two_ways(a, 0, lambda d: cur_ref.at[a, rows16(u + 2, d)], lambda d: a1_ref.at[a, d])
        if n == 1:
            return two_ways(a, 1, lambda d: cur_ref.at[a, rows32(u + 1 - 2 * d)], lambda d: a2_ref.at[a, d])
        if n == 2:
            return [
                remote(
                    cur_ref.at[a, rows32(u), cols(v + by)], b_ref.at[a, by - 1],
                    b_send.at[a, 0, by - 1], b_recv.at[a, 0, by - 1], near(second, by),
                )
                for by in (1, 2, 3)
            ]
        if n == 3:
            block = blk_ref.at[a, :, cols(v)]
            return [
                remote(block, block, b_send.at[a, 1, by - 1], b_recv.at[a, 1, by - 1], near(second, by))
                for by in (1, 2, 3)
            ]
        if n == 4:
            block = mine.at[rows32(u)]
            return two_ways(a, 2, lambda d: block, lambda d: block)

        def half(d):
            return mine.at[rows16(u - 1 + 2 * d, d)]

        return two_ways(a, 3, half, half)

    def pair_copy(a):
        return remote(send_ref.at[a], got_ref.at[a], pair_send.at[0, a], pair_recv.at[0, a], sibling)

    def give_copy(a, which):
        here = out_ref.at[which, a]
        return remote(here, here, pair_send.at[1, a], pair_recv.at[1, a], sibling)

    def loads(a):
        return [
            pltpu.make_async_copy(left_hbm.at[a], left_ref.at[a], load_sem.at[0, a]),
            pltpu.make_async_copy(right_hbm.at[a], right_ref.at[a], load_sem.at[1, a]),
            pltpu.make_async_copy(probe_hbm.at[a], probe_ref.at[a], load_sem.at[2, a]),
        ]

    def start(a, n):
        for copy in copies(a, n):
            copy.start()

    def arrive(a, n):
        for copy in copies(a, n):
            copy.wait_recv()

    def compute(a):
        column = step_ref[0]
        for copy in loads(a):
            copy.wait()
        level = lax.broadcasted_iota(jnp.int32, (128, 96), 1)
        live = z * 6 + a > column
        range_sum = jnp.zeros((128, 512), F32)
        co_sum = jnp.zeros((128, 512), F32)
        for j in range(3):
            tile = c * 3 + j
            own = tile == column
            depth = jnp.where(live & (tile <= column), ranks_ref[j, a], 0)
            keep = level < depth
            left = left_ref[a, j]
            right = right_ref[a, j]
            both = dot_nt(stack_ref[j], right)
            coupled = both[:96].astype(BF16)
            mixed = dot_nn(reduced_ref[j], coupled)
            mixed = jnp.where(own, -both[96:], mixed)
            mixed = jnp.where(keep, mixed, 0.0).astype(BF16)
            probed = dot_nt(probe_ref[a], left)
            probed = jnp.where(keep, probed, 0.0).astype(BF16)
            folded = dot_nt(probed, coupled).astype(BF16)
            folded = jnp.where(own, -probed, folded)
            closing = jnp.where(own, right, upper_ref[j, 1])
            range_sum += dot_nn(mixed, left)
            co_sum += dot_nn(folded, closing)
        even = core == 0
        acc_ref[a] = -jnp.where(even, range_sum, co_sum)
        send_ref[a] = -jnp.where(even, co_sum, range_sum).astype(BF16)
        pair_copy(a).start()

    def stage(n, a):
        first, second = axes(a)
        u, v = place[first], place[second]
        if n == 0:
            pair_copy(a).wait_recv()
            acc_ref[a] += got_ref[a].astype(F32)
            cur_ref[a, rows32(u + 2)] = acc_ref[a, rows32(u + 2)].astype(BF16)
            start(a, 0)
        elif n == 1:
            arrive(a, 0)
            for d in range(2):
                near_rows = rows32(u + 1 - 2 * d)
                rows = rows16(u + 1 - 2 * d, d)
                acc_ref[a, rows] += a1_ref[a, d].astype(F32)
                cur_ref[a, near_rows] = acc_ref[a, near_rows].astype(BF16)
            start(a, 1)
        elif n == 2:
            arrive(a, 1)
            rows = rows32(u)
            total = acc_ref[a, rows] + a2_ref[a, 0].astype(F32) + a2_ref[a, 1].astype(F32)
            acc_ref[a, rows] = total
            cur_ref[a, rows] = total.astype(BF16)
            start(a, 2)
        elif n == 3:
            arrive(a, 2)
            total = acc_ref[a, rows32(u), cols(v)]
            for d in range(3):
                total += b_ref[a, d].astype(F32)
            blk_ref[a, :, cols(v)] = total.astype(BF16)
            start(a, 3)
        elif n == 4:
            for by in (1, 2, 3):
                theirs = blk_ref.at[a, :, cols(v - by)]
                remote(
                    theirs, theirs, b_send.at[a, 1, by - 1], b_recv.at[a, 1, by - 1], near(second, by)
                ).wait_recv()

            @pl.when(core == 0)
            def _():
                out_ref[0, a, rows32(u)] = blk_ref[a]

            @pl.when(core == 1)
            def _():
                out_ref[1, a, rows32(u)] = dot_nn(blk_ref[a], solve_ref[...]).astype(BF16)

            start(a, 4)
        elif n == 5:
            arrive(a, 4)
            start(a, 5)
        elif n == 6:
            arrive(a, 5)
            give_copy(a, core).start()
        else:
            give_copy(a, 1 - core).wait_recv()

    @pl.when(z < FIRST)
    def _():
        out_ref[...] = jnp.zeros_like(out_ref)

    @pl.when(z >= FIRST)
    def _():
        for a in order:
            for copy in loads(a):
                copy.start()
        barrier = pltpu.get_barrier_semaphore()
        peers = (sibling, near(0, 1), near(0, 2), near(0, 3), near(1, 1), near(1, 2), near(1, 3))
        for device in peers:
            pl.semaphore_signal(barrier, inc=1, device_id=device, device_id_type=MESH)
        flat = sketch_ref[...].astype(F32).T.astype(BF16)
        for j in range(3):
            stack_ref[j, :96] = upper_ref[j, 0]
            stack_ref[j, 96:] = flat
            reduced = dot_nn(upper_ref[j, 1], sketch_ref[...]).astype(BF16).astype(F32)
            reduced_ref[j] = reduced.T.astype(BF16)
        pl.semaphore_wait(barrier, 7)
        for t in range(15):
            if t < 6:
                compute(order[t])
            for n in reversed(range(8)):
                if 0 <= t - 1 - n < 6:
                    stage(n, order[t - 1 - n])
        for a in range(6):
            pair_copy(a).wait_send()
            give_copy(a, core).wait_send()
            for n in range(6):
                for copy in copies(a, n):
                    copy.wait_send()


def row_sums(ranks, step, left, right, probes, upper, sketch, solve):
    vmem = pl.BlockSpec(memory_space=pltpu.VMEM)
    smem = pl.BlockSpec(memory_space=pltpu.SMEM)
    hbm = pl.BlockSpec(memory_space=pl.ANY)
    return pl.pallas_call(
        row_kernel,
        out_shape=jax.ShapeDtypeStruct((2, 6, 128, 512), BF16),
        in_specs=[smem, smem, hbm, hbm, hbm, vmem, vmem, vmem],
        out_specs=vmem,
        scratch_shapes=[
            pltpu.VMEM((6, 3, 96, 512), BF16),
            pltpu.VMEM((6, 3, 96, 512), BF16),
            pltpu.VMEM((6, 128, 512), BF16),
            pltpu.VMEM((3, 224, 512), BF16),
            pltpu.VMEM((3, 128, 96), BF16),
            pltpu.VMEM((6, 128, 512), BF16),
            pltpu.VMEM((6, 128, 512), BF16),
            pltpu.VMEM((6, 128, 512), F32),
            pltpu.VMEM((6, 128, 512), BF16),
            pltpu.VMEM((6, 2, 16, 512), BF16),
            pltpu.VMEM((6, 2, 32, 512), BF16),
            pltpu.VMEM((6, 3, 32, 128), BF16),
            pltpu.VMEM((6, 32, 512), BF16),
            pltpu.SemaphoreType.DMA((3, 6)),
            pltpu.SemaphoreType.DMA((6, 4, 2)),
            pltpu.SemaphoreType.DMA((6, 4, 2)),
            pltpu.SemaphoreType.DMA((6, 2, 3)),
            pltpu.SemaphoreType.DMA((6, 2, 3)),
            pltpu.SemaphoreType.DMA((2, 6)),
            pltpu.SemaphoreType.DMA((2, 6)),
        ],
        compiler_params=pltpu.CompilerParams(
            collective_id=0, has_side_effects=True, vmem_limit_bytes=62 * 2**20
        ),
        name="row_sums",
    )(ranks, step, left, right, probes, upper, sketch, solve)


def body(left_factors, right_factors, ranks, sketch_left, sketch_right, upper_inverse, step):
    slots = ranks.T
    panel = gather_panel(slots, step, left_factors, right_factors)
    branches = [functools.partial(spread_panel, owner) for owner in range(16, 32)]
    upper = lax.switch(lax.div(step[0], 3) - 16, branches, panel)
    out = row_sums(
        slots, step, left_factors, right_factors, sketch_left, upper, sketch_right, upper_inverse
    )
    return (out[0], out[1])


def solution(mesh):
    return jax.shard_map(
        body,
        mesh=mesh,
        in_specs=(
            P("row", "col", None, None),
            P("row", "col", None, None),
            P("row", "col"),
            P("row", None, None),
            P(),
            P(),
            P(),
        ),
        out_specs=(P("row", None, None), P("row", None, None)),
        check_vma=False,
    )
```

time: 466 us -> 102 us (0.22)
  the two profiles are of different devices: /device:TPU:32 before, /device:TPU:481 now
where the time goes in v1:
time: 102 us; the launch traced here: 101 us
  Pallas kernels  97.3 us (95%)
  local copies, waits for them, and re-layouts  2.61 us (3%)
  between operations  1.31 us (1%)
    pallas_call x1, Pallas kernels, row_sums(): pl.pallas_call(row_kernel, out_shape=jax.ShapeDtypeStruct((2, 6, 128, 512...  73.8 us
    pallas_call x1, Pallas kernels, spread_panel(): pl.pallas_call(functools.partial(panel_kernel, owner), out_shape=jax.Shap...  22.7 us
    squeeze x1, local copies, waits for them, and re-layouts, body(): return (out[0], out[1])  2.61 us

profile of v1, /device:TPU:481, one launch (start us, length us, event | category | flops | bytes accessed | tf_op | source)
XLA Modules:
  0.0 101.3 jit_solution(13532358553930834153)
XLA Ops:
  1.3 0.7 gather_panel.1
  2.0 22.8 %conditional.1 = (bf16[3,2,96,512]{3,2,1,0:T(8,128)(2,1)S(1)}) conditional(s32[]{:T(128)} %bitcast.1, bf16[6,2,96,512]{3,2,1,0:T(8,128)(2,1)S(1)} %gather_panel.1, bf16[6,2,96,512]{3,2,1,0:T(8,128)(2,1)S(1)} %gather_panel.1, bf16[6,2,96,512]{3,2,1,0:T(8,128)(2,1)S(1)} %gather_panel.1, ...), branch_computations={%region_0.0_spmd, %region_1.0_spmd, %region_2.0_spmd, %region_3.0_... | conditional | bytes 8 | solution.py:511
  2.1 22.7 %spread_panel.21 = bf16[3,2,96,512]{3,2,1,0:T(8,128)(2,1)S(1)} custom-call(bf16[6,2,96,512]{3,2,1,0:T(8,128)(2,1)S(1)} %panel_ref.5), custom_call_target="tpu_custom_call" | custom-call | tf_op jit(solution)/shard_map/cond/branch_5_fun/spread_panel/pallas_call | solution.py:224
  24.8 73.8 %row_sums.1 = bf16[2,6,128,512]{3,2,1,0:T(8,128)(2,1)} custom-call(s32[3,6]{1,0:T(4,128)} %bitcast.7, s32[1]{0:T(128)S(6)} %copy.25.step_ref, bf16[6,3,96,512]{3,2,1,0:T(8,128)(2,1)} %left_hbm.1, bf16[6,3,96,512]{3,2,1,0:T(8,128)(2,1)} %right_hbm.1, bf16[6,128,512]{2,1,0:T(8,128)(2,1)} %probe_hbm.1, bf16[3,2,96,512]{3,2,1,0:T(8,128)(2,1)S(1)} %get-tuple-element.37.upper_ref, ...), custom_call_target="tpu_custom_call" | custom-call | tf_op jit(solution)/shard_map/row_sums/pallas_call | solution.py:473
  98.7 2.6 %slice_bitcast_fusion = (bf16[6,128,512]{2,1,0:T(8,128)(2,1)}, bf16[6,128,512]{2,1,0:T(8,128)(2,1)}) fusion(bf16[2,6,128,512]{3,2,1,0:T(8,128)(2,1)} %row_sums.1), kind=kLoop, calls=%fused_computation | loop fusion | bytes 3145728 | tf_op jit(solution)/shard_map/squeeze | solution.py:515

commit v2 on v1

--- a/solution.py
+++ b/solution.py
@@ -25,6 +25,72 @@
         device_id=device,
         device_id_type=MESH,
     )
+
+
+def line_trees():
+    trees = []
+    for s in range(16):
+        parent = {}
+
+        def chain(*planes):
+            for before, after in zip(planes, planes[1:]):
+                parent[after] = before
+
+        low = s < FIRST
+        if low or s == 15:
+            chain(*((s, 4, 9) if s < 2 else (s, 5, 9) if s == 15 else (s, 9)), 10, 11)
+            chain(9, 8)
+        if low or s == 8:
+            chain(*((s, 3, 14) if 6 <= s < 8 else (s, 2, 14) if s == 8 else (s, 14)), 13, 12)
+            chain(14, 15)
+        if s == 8:
+            chain(8, 9, 10, 11)
+        if s == 15:
+            chain(15, 14, 13, 12)
+        if s == 9:
+            chain(9, 10, 11, 12, 13)
+            chain(9, 8, 2, 15, 14)
+        if s == 14:
+            chain(14, 13, 12, 11, 10)
+            chain(14, 15, 5, 8, 9)
+        if 10 <= s <= 13:
+            chain(*range(s, 16))
+            chain(*range(s, 7, -1))
+        trees.append(parent)
+    return trees
+
+
+def table_words(entries):
+    return [
+        sum(entries[s][4 * w + d] * 16**d for d in range(4)) for s in range(16) for w in range(4)
+    ]
+
+
+def tree_tables():
+    none = [list(range(16)) for _ in range(16)]
+    parents = [list(row) for row in none]
+    firsts = [list(row) for row in none]
+    seconds = [list(row) for row in none]
+    for s, tree in enumerate(line_trees()):
+        for plane, before in tree.items():
+            parents[s][plane] = before
+            if firsts[s][before] == before:
+                firsts[s][before] = plane
+            else:
+                assert seconds[s][before] == before
+                seconds[s][before] = plane
+    return [table_words(entries) for entries in (parents, firsts, seconds)]
+
+
+def look_up(words, s, z):
+    index = s * 4 + z // 4
+    word = words[0]
+    for k, value in enumerate(words):
+        if k:
+            word = jnp.where(index == k, value, word)
+    digit = z % 4
+    scale = jnp.where(digit == 0, 1, jnp.where(digit == 1, 16, jnp.where(digit == 2, 256, 4096)))
+    return (word // scale) % 16
 
 
 def gather_kernel(ranks_ref, step_ref, left_ref, right_ref, panel_ref, sems):
@@ -66,7 +132,7 @@
 
 def panel_kernel(
     owner, panel_ref, out_ref, extra_ref, src_send, up_send, down_send, recv_sem,
-    extra_up, extra_down, extra_recv, give_send, local_sem,
+    extra_up_send, extra_down_send, extra_recv, give_send, local_sem,
 ):
     z = lax.axis_index("row")
     c = lax.axis_index("col")
@@ -75,32 +141,24 @@
     owner_line = owner // 2
     owner_core = owner % 2
     carrier = owner + 1 - 2 * owner_core
-    low = s < FIRST
-    high = jnp.logical_not(low)
     home = z == s
     is_owner = c == owner
     is_carrier = c == carrier
     target = z >= FIRST
-    way = (c == 0) & (z == 4)
-    up = (low & (kind == 0) & (home | way | (target & (z < LAST)))) | (high & (z >= s) & (z < LAST))
-    down = (low & (kind == 1) & (home | (z > FIRST))) | (high & (z <= s) & (z > FIRST))
-    up = up & jnp.logical_not(is_owner)
-    down = down & jnp.logical_not(is_owner)
-    up_to = jnp.where((c == 0) & (z == 0), 4, jnp.where(z < FIRST, FIRST, z + 1))
-    down_to = jnp.where(z < FIRST, LAST, z - 1)
-    from_owner = home & jnp.logical_not(is_owner)
-    from_below = ((low & (kind == 0)) | (high & (z > s))) & target | way
-    from_above = ((low & (kind == 1)) | (high & (z < s))) & target
-    from_below = from_below & jnp.logical_not(is_owner)
-    from_above = from_above & jnp.logical_not(is_owner)
-    entry = jnp.where(c == 0, 4, s)
-    below = jnp.where(way, 0, jnp.where(low & (z == FIRST), entry, z - 1))
-    above = jnp.where(low & (z == LAST), s, z + 1)
+    parent, first, second = (look_up(words, s, z) for words in tree_tables())
+    plain = jnp.logical_not(is_owner)
+    up = plain & (first != z)
+    down = plain & (second != z)
+    from_owner = home & plain
+    from_parent = plain & (parent != z)
     from_carrier = is_owner & target & (z != owner_line)
-    receives = from_owner | from_below | from_above | from_carrier
+    receives = from_owner | from_parent | from_carrier
     sends_home = is_owner & (z != owner_line)
     holds_own = is_owner & (z == owner_line)
-    carries = is_carrier & target
+    extra_up = is_carrier & (first != z)
+    extra_down = is_carrier & (second != z)
+    extra_gives = is_carrier & target & (z != owner_line)
+    extra_takes = is_carrier & (home | (parent != z))
 
     barrier = pltpu.get_barrier_semaphore()
 
@@ -110,8 +168,7 @@
             pl.semaphore_signal(barrier, inc=1, device_id=device, device_id_type=MESH)
 
     greet(from_owner, (z, owner))
-    greet(from_below, (below, c))
-    greet(from_above, (above, c))
+    greet(from_parent, (parent, c))
     greet(from_carrier, (z, carrier))
 
     def count(flag, amount=1):
@@ -121,7 +178,7 @@
         count(is_owner, jnp.where(z == owner_line, 1, 2))
         + count(up)
         + count(down)
-        + count(carries & (z != owner_line))
+        + count(extra_gives)
     )
 
     @pl.when(peers > 0)
@@ -163,16 +220,16 @@
         )
 
     def up_copy(q):
-        return chain_copy(out_ref, up_send, recv_sem, (up_to, c), q)
+        return chain_copy(out_ref, up_send, recv_sem, (first, c), q)
 
     def down_copy(q):
-        return chain_copy(out_ref, down_send, recv_sem, (down_to, c), q)
+        return chain_copy(out_ref, down_send, recv_sem, (second, c), q)
 
     def extra_up_copy(q):
-        return chain_copy(extra_ref, extra_up, extra_recv, (z + 1, c), q)
+        return chain_copy(extra_ref, extra_up_send, extra_recv, (first, c), q)
 
     def extra_down_copy(q):
-        return chain_copy(extra_ref, extra_down, extra_recv, (z - 1, c), q)
+        return chain_copy(extra_ref, extra_down_send, extra_recv, (second, c), q)
 
     def loop(flag, body):
         @pl.when(flag)
@@ -200,12 +257,12 @@
         when(up, lambda: up_copy(q).start())
         when(down, lambda: down_copy(q).start())
 
-        @pl.when(carries)
+        @pl.when(extra_takes)
         def _():
-            chain_copy(extra_ref, extra_up, extra_recv, (z, owner), q).wait_recv()
-            when((z >= owner_line) & (z < LAST), lambda: extra_up_copy(q).start())
-            when((z <= owner_line) & (z > FIRST), lambda: extra_down_copy(q).start())
-            when(z != owner_line, lambda: give_copy(q).start())
+            chain_copy(extra_ref, extra_up_send, extra_recv, (z, owner), q).wait_recv()
+            when(extra_up, lambda: extra_up_copy(q).start())
+            when(extra_down, lambda: extra_down_copy(q).start())
+            when(extra_gives, lambda: give_copy(q).start())
 
     lax.fori_loop(0, CHUNKS, lambda q, _: (relay(q), 0)[1], 0)
 
@@ -215,9 +272,9 @@
         loop(flag, lambda q, core=core: src_copy(core, q).wait_send())
     loop(up, lambda q: up_copy(q).wait_send())
     loop(down, lambda q: down_copy(q).wait_send())
-    loop(carries & (z >= owner_line) & (z < LAST), lambda q: extra_up_copy(q).wait_send())
-    loop(carries & (z <= owner_line) & (z > FIRST), lambda q: extra_down_copy(q).wait_send())
-    loop(carries & (z != owner_line), lambda q: give_copy(q).wait_send())
+    loop(extra_up, lambda q: extra_up_copy(q).wait_send())
+    loop(extra_down, lambda q: extra_down_copy(q).wait_send())
+    loop(extra_gives, lambda q: give_copy(q).wait_send())
 
 
 def spread_panel(owner, panel):
@@ -256,8 +313,8 @@
 def row_kernel(
     ranks_ref, step_ref, left_hbm, right_hbm, probe_hbm, upper_ref, sketch_ref, solve_ref, out_ref,
     left_ref, right_ref, probe_ref, stack_ref, reduced_ref,
-    send_ref, got_ref, acc_ref, cur_ref, a1_ref, a2_ref, b_ref, blk_ref,
-    load_sem, send_sem, recv_sem, b_send, b_recv, pair_send, pair_recv,
+    send_ref, got_ref, acc_ref, cur_ref, a_ref, b_ref, blk_ref,
+    load_sem, send_sem, recv_sem, pair_send, pair_recv,
 ):
     z = lax.axis_index("row")
     c = lax.axis_index("col")
@@ -265,63 +322,57 @@
     y = (c // 2) % 4
     core = c % 2
     sibling = (z, c + 1 - 2 * core)
-    place = (x, y)
-    order = (0, 3, 1, 4, 2, 5)
 
     def near(axis, by):
-        if axis == 0:
-            return (z, ((x + by + 4) % 4) * 8 + y * 2 + core)
-        return (z, x * 8 + ((y + by + 4) % 4) * 2 + core)
+        beside = ((x + by) % 4) * 8 + y * 2 + core
+        above = x * 8 + ((y + by) % 4) * 2 + core
+        return (z, jnp.where(axis == 0, beside, above))
 
     def rows32(b):
         return pl.ds(pl.multiple_of(((b + 4) % 4) * 32, 32), 32)
 
-    def rows16(b, h):
-        return pl.ds(pl.multiple_of(((b + 4) % 4) * 32 + 16 * h, 16), 16)
-
     def cols(b):
         return pl.ds(pl.multiple_of(((b + 4) % 4) * 128, 128), 128)
 
-    def axes(a):
-        return (0, 1) if a < 3 else (1, 0)
-
-    def two_ways(a, n, src, dst):
-        axis = axes(a)[0]
-        return [
-            remote(src(d), dst(d), send_sem.at[a, n, d], recv_sem.at[a, n, d], near(axis, 1 - 2 * d))
-            for d in range(2)
-        ]
+    def spot(a):
+        first = a % 2
+        return first, 1 - first, jnp.where(first == 0, x, y), jnp.where(first == 0, y, x)
 
     def copies(a, n):
-        first, second = axes(a)
-        u, v = place[first], place[second]
-        mine = out_ref.at[core, a]
-        if n == 0:
-            return two_ways(a, 0, lambda d: cur_ref.at[a, rows16(u + 2, d)], lambda d: a1_ref.at[a, d])
-        if n == 1:
-            return two_ways(a, 1, lambda d: cur_ref.at[a, rows32(u + 1 - 2 * d)], lambda d: a2_ref.at[a, d])
-        if n == 2:
-            return [
-                remote(
-                    cur_ref.at[a, rows32(u), cols(v + by)], b_ref.at[a, by - 1],
-                    b_send.at[a, 0, by - 1], b_recv.at[a, 0, by - 1], near(second, by),
-                )
-                for by in (1, 2, 3)
-            ]
-        if n == 3:
-            block = blk_ref.at[a, :, cols(v)]
-            return [
-                remote(block, block, b_send.at[a, 1, by - 1], b_recv.at[a, 1, by - 1], near(second, by))
-                for by in (1, 2, 3)
-            ]
-        if n == 4:
-            block = mine.at[rows32(u)]
-            return two_ways(a, 2, lambda d: block, lambda d: block)
-
-        def half(d):
-            return mine.at[rows16(u - 1 + 2 * d, d)]
-
-        return two_ways(a, 3, half, half)
+        first, second, u, v = spot(a)
+        made = []
+        for by in (1, 2, 3):
+            if n == 0:
+                src, dst = cur_ref.at[a, rows32(u + by)], a_ref.at[a, by - 1]
+            elif n == 1:
+                src, dst = cur_ref.at[a, rows32(u), cols(v + by)], b_ref.at[a, by - 1]
+            elif n == 2:
+                src = dst = blk_ref.at[a, :, cols(v)]
+            else:
+                src = dst = out_ref.at[core, a, rows32(u)]
+            axis = first if n in (0, 3) else second
+            sem = (a, n, by - 1)
+            made.append(remote(src, dst, send_sem.at[sem], recv_sem.at[sem], near(axis, by)))
+        return made
+
+    def start(a, n):
+        for copy in copies(a, n):
+            copy.start()
+
+    def arrive(a, n):
+        first, second, u, v = spot(a)
+        for by in (1, 2, 3):
+            if n == 0:
+                dst = a_ref.at[a, by - 1]
+            elif n == 1:
+                dst = b_ref.at[a, by - 1]
+            elif n == 2:
+                dst = blk_ref.at[a, :, cols(v - by)]
+            else:
+                dst = out_ref.at[core, a, rows32(u - by)]
+            axis = first if n in (0, 3) else second
+            sem = (a, n, by - 1)
+            remote(dst, dst, send_sem.at[sem], recv_sem.at[sem], near(axis, by)).wait_recv()
 
     def pair_copy(a):
         return remote(send_ref.at[a], got_ref.at[a], pair_send.at[0, a], pair_recv.at[0, a], sibling)
@@ -336,14 +387,6 @@
             pltpu.make_async_copy(right_hbm.at[a], right_ref.at[a], load_sem.at[1, a]),
             pltpu.make_async_copy(probe_hbm.at[a], probe_ref.at[a], load_sem.at[2, a]),
         ]
-
-    def start(a, n):
-        for copy in copies(a, n):
-            copy.start()
-
-    def arrive(a, n):
-        for copy in copies(a, n):
-            copy.wait_recv()
 
     def compute(a):
         column = step_ref[0]
@@ -378,41 +421,35 @@
         pair_copy(a).start()
 
     def stage(n, a):
-        first, second = axes(a)
-        u, v = place[first], place[second]
+        first, second, u, v = spot(a)
         if n == 0:
             pair_copy(a).wait_recv()
-            acc_ref[a] += got_ref[a].astype(F32)
-            cur_ref[a, rows32(u + 2)] = acc_ref[a, rows32(u + 2)].astype(BF16)
+            for by in range(4):
+                rows = rows32(u + by)
+                total = acc_ref[a, rows] + got_ref[a, rows].astype(F32)
+                if by:
+                    cur_ref[a, rows] = total.astype(BF16)
+                else:
+                    acc_ref[a, rows] = total
             start(a, 0)
         elif n == 1:
             arrive(a, 0)
-            for d in range(2):
-                near_rows = rows32(u + 1 - 2 * d)
-                rows = rows16(u + 1 - 2 * d, d)
-                acc_ref[a, rows] += a1_ref[a, d].astype(F32)
-                cur_ref[a, near_rows] = acc_ref[a, near_rows].astype(BF16)
+            rows = rows32(u)
+            total = acc_ref[a, rows]
+            for d in range(3):
+                total += a_ref[a, d].astype(F32)
+            acc_ref[a, rows] = total
+            cur_ref[a, rows] = total.astype(BF16)
             start(a, 1)
         elif n == 2:
             arrive(a, 1)
-            rows = rows32(u)
-            total = acc_ref[a, rows] + a2_ref[a, 0].astype(F32) + a2_ref[a, 1].astype(F32)
-            acc_ref[a, rows] = total
-            cur_ref[a, rows] = total.astype(BF16)
-            start(a, 2)
-        elif n == 3:
-            arrive(a, 2)
             total = acc_ref[a, rows32(u), cols(v)]
             for d in range(3):
                 total += b_ref[a, d].astype(F32)
             blk_ref[a, :, cols(v)] = total.astype(BF16)
-            start(a, 3)
-        elif n == 4:
-            for by in (1, 2, 3):
-                theirs = blk_ref.at[a, :, cols(v - by)]
-                remote(
-                    theirs, theirs, b_send.at[a, 1, by - 1], b_recv.at[a, 1, by - 1], near(second, by)
-                ).wait_recv()
+            start(a, 2)
+        elif n == 3:
+            arrive(a, 2)
 
             @pl.when(core == 0)
             def _():
@@ -422,12 +459,9 @@
             def _():
                 out_ref[1, a, rows32(u)] = dot_nn(blk_ref[a], solve_ref[...]).astype(BF16)
 
-            start(a, 4)
-        elif n == 5:
-            arrive(a, 4)
-            start(a, 5)
-        elif n == 6:
-            arrive(a, 5)
+            start(a, 3)
+        elif n == 4:
+            arrive(a, 3)
             give_copy(a, core).start()
         else:
             give_copy(a, 1 - core).wait_recv()
@@ -438,7 +472,7 @@
 
     @pl.when(z >= FIRST)
     def _():
-        for a in order:
+        for a in range(6):
             for copy in loads(a):
                 copy.start()
         barrier = pltpu.get_barrier_semaphore()
@@ -452,18 +486,32 @@
             reduced = dot_nn(upper_ref[j, 1], sketch_ref[...]).astype(BF16).astype(F32)
             reduced_ref[j] = reduced.T.astype(BF16)
         pl.semaphore_wait(barrier, 7)
-        for t in range(15):
-            if t < 6:
-                compute(order[t])
-            for n in reversed(range(8)):
-                if 0 <= t - 1 - n < 6:
-                    stage(n, order[t - 1 - n])
-        for a in range(6):
+
+        def slot(t, _):
+            @pl.when(t < 6)
+            def _():
+                compute(t)
+
+            for n in reversed(range(6)):
+                a = t - 1 - n
+
+                @pl.when((a >= 0) & (a < 6))
+                def _(n=n, a=a):
+                    stage(n, a)
+
+            return 0
+
+        lax.fori_loop(0, 12, slot, 0)
+
+        def finish(a, _):
             pair_copy(a).wait_send()
             give_copy(a, core).wait_send()
-            for n in range(6):
+            for n in range(4):
                 for copy in copies(a, n):
                     copy.wait_send()
+            return 0
+
+        lax.fori_loop(0, 6, finish, 0)
 
 
 def row_sums(ranks, step, left, right, probes, upper, sketch, solve):
@@ -485,20 +533,17 @@
             pltpu.VMEM((6, 128, 512), BF16),
             pltpu.VMEM((6, 128, 512), F32),
             pltpu.VMEM((6, 128, 512), BF16),
-            pltpu.VMEM((6, 2, 16, 512), BF16),
-            pltpu.VMEM((6, 2, 32, 512), BF16),
+            pltpu.VMEM((6, 3, 32, 512), BF16),
             pltpu.VMEM((6, 3, 32, 128), BF16),
             pltpu.VMEM((6, 32, 512), BF16),
             pltpu.SemaphoreType.DMA((3, 6)),
-            pltpu.SemaphoreType.DMA((6, 4, 2)),
-            pltpu.SemaphoreType.DMA((6, 4, 2)),
-            pltpu.SemaphoreType.DMA((6, 2, 3)),
-            pltpu.SemaphoreType.DMA((6, 2, 3)),
+            pltpu.SemaphoreType.DMA((6, 4, 3)),
+            pltpu.SemaphoreType.DMA((6, 4, 3)),
             pltpu.SemaphoreType.DMA((2, 6)),
             pltpu.SemaphoreType.DMA((2, 6)),
         ],
         compiler_params=pltpu.CompilerParams(
-            collective_id=0, has_side_effects=True, vmem_limit_bytes=62 * 2**20
+            collective_id=0, has_side_effects=True, vmem_limit_bytes=50 * 2**20
         ),
         name="row_sums",
     )(ranks, step, left, right, probes, upper, sketch, solve)

time: 102 us -> 90.3 us (0.89)
  Pallas kernels: 97.3 us -> 86.2 us
  local copies, waits for them, and re-layouts: 2.61 us -> 1.27 us
    pallas_call x1, Pallas kernels: 73.8 us -> 59.5 us  [row_sums(): pl.pallas_call(row_kernel, out_shape=jax.ShapeDtypeStruct((2, 6, 128, 512...]
    pallas_call x1, Pallas kernels: 22.7 us -> 26 us  [spread_panel(): pl.pallas_call(functools.partial(panel_kernel, owner), out_shape=jax.Shap...]
    squeeze x1, local copies, waits for them, and re-layouts: 2.61 us -> 1.24 us  [body(): return (out[0], out[1])]
where the time goes in v2:
time: 90.3 us; the launch traced here: 88.9 us
  Pallas kernels  86.2 us (95%)
  between operations  1.37 us (2%)
  local copies, waits for them, and re-layouts  1.27 us (1%)
    pallas_call x1, Pallas kernels, row_sums(): pl.pallas_call(row_kernel, out_shape=jax.ShapeDtypeStruct((2, 6, 128, 512...  59.5 us
    pallas_call x1, Pallas kernels, spread_panel(): pl.pallas_call(functools.partial(panel_kernel, owner), out_shape=jax.Shap...  26 us

profile of v2, /device:TPU:481, one launch (start us, length us, event | category | flops | bytes accessed | tf_op | source)
XLA Modules:
  0.0 88.9 jit_solution(17895267230237574527)
XLA Ops:
  1.3 0.7 gather_panel.1
  2.0 0.0 copy-start
  2.0 0.0 copy-start.1
  2.0 0.0 copy-start.2
  2.1 0.0 copy-start.3
  2.1 26.1 %conditional.1 = (bf16[3,2,96,512]{3,2,1,0:T(8,128)(2,1)S(1)}) conditional(s32[]{:T(128)} %bitcast.1, bf16[6,2,96,512]{3,2,1,0:T(8,128)(2,1)S(1)} %gather_panel.1, bf16[6,2,96,512]{3,2,1,0:T(8,128)(2,1)S(1)} %gather_panel.1, bf16[6,2,96,512]{3,2,1,0:T(8,128)(2,1)S(1)} %gather_panel.1, ...), branch_computations={%region_0.0_spmd, %region_1.0_spmd, %region_2.0_spmd, %region_3.0_... | conditional | bytes 8 | solution.py:556
  2.1 26.0 %spread_panel.23 = bf16[3,2,96,512]{3,2,1,0:T(8,128)(2,1)S(1)} custom-call(bf16[6,2,96,512]{3,2,1,0:T(8,128)(2,1)S(1)} %panel_ref.7), custom_call_target="tpu_custom_call" | custom-call | tf_op jit(solution)/shard_map/cond/branch_7_fun/spread_panel/pallas_call | solution.py:281
  28.2 0.0 copy-done
  28.2 0.0 copy-done.1
  28.2 0.0 copy-done.2
  28.2 0.0 copy-done.3
  28.2 59.5 %row_sums.1 = bf16[2,6,128,512]{3,2,1,0:T(8,128)(2,1)S(1)} custom-call(s32[3,6]{1,0:T(4,128)S(1)} %bitcast.7, s32[1]{0:T(128)S(6)} %copy.25.step_ref, bf16[6,3,96,512]{3,2,1,0:T(8,128)(2,1)} %left_hbm.1, bf16[6,3,96,512]{3,2,1,0:T(8,128)(2,1)} %right_hbm.1, bf16[6,128,512]{2,1,0:T(8,128)(2,1)S(1)} %copy-done, ...), custom_call_target="tpu_custom_call" | custom-call | tf_op jit(solution)/shard_map/row_sums/pallas_call | solution.py:521
  87.7 1.2 %slice_bitcast_fusion = (bf16[6,128,512]{2,1,0:T(8,128)(2,1)}, bf16[6,128,512]{2,1,0:T(8,128)(2,1)}) fusion(bf16[2,6,128,512]{3,2,1,0:T(8,128)(2,1)S(1)} %row_sums.1), kind=kLoop, calls=%fused_computation | loop fusion | bytes 3145728 | tf_op jit(solution)/shard_map/squeeze | solution.py:560
Async XLA Ops:
  2.0 26.1 %copy-start = (bf16[6,128,512]{2,1,0:T(8,128)(2,1)S(1)}, bf16[6,128,512]{2,1,0:T(8,128)(2,1)}, u32[]{:S(2)}) copy-start(bf16[6,128,512]{2,1,0:T(8,128)(2,1)} %probe_hbm.1) | copy-start | bytes 2359300
  2.0 26.1 %copy-start.1 = (bf16[512,512]{1,0:T(8,128)(2,1)S(1)}, bf16[512,512]{1,0:T(8,128)(2,1)}, u32[]{:S(2)}) copy-start(bf16[512,512]{1,0:T(8,128)(2,1)} %solve_ref.1) | copy-start | bytes 1572868
  2.0 26.1 %copy-start.2 = (bf16[512,128]{1,0:T(8,128)(2,1)S(1)}, bf16[512,128]{1,0:T(8,128)(2,1)}, u32[]{:S(2)}) copy-start(bf16[512,128]{1,0:T(8,128)(2,1)} %sketch_ref.1) | copy-start | bytes 393220
  2.1 26.1 %copy-start.3 = (s32[6,3]{0,1:T(4,128)S(1)}, s32[6,3]{0,1:T(4,128)}, u32[]{:S(2)}) copy-start(s32[6,3]{0,1:T(4,128)} %param.25) | copy-start | bytes 220

commit v3 on v2

--- a/solution.py
+++ b/solution.py
@@ -310,10 +310,14 @@
     return jnp.dot(a, b, preferred_element_type=F32)
 
 
+GROUP = 2
+GROUPS = 6 // GROUP
+
+
 def row_kernel(
     ranks_ref, step_ref, left_hbm, right_hbm, probe_hbm, upper_ref, sketch_ref, solve_ref, out_ref,
     left_ref, right_ref, probe_ref, stack_ref, reduced_ref,
-    send_ref, got_ref, acc_ref, cur_ref, a_ref, b_ref, blk_ref,
+    send_ref, got_ref, acc_ref, cur_ref, a_ref, b_ref,
     load_sem, send_sem, recv_sem, pair_send, pair_recv,
 ):
     z = lax.axis_index("row")
@@ -321,150 +325,147 @@
     x = c // 8
     y = (c // 2) % 4
     core = c % 2
+    even = core == 0
     sibling = (z, c + 1 - 2 * core)
-
-    def near(axis, by):
-        beside = ((x + by) % 4) * 8 + y * 2 + core
-        above = x * 8 + ((y + by) % 4) * 2 + core
-        return (z, jnp.where(axis == 0, beside, above))
+    u = jnp.where(even, x, y)
+    v = jnp.where(even, y, x)
+
+    def along_x(by):
+        return ((x + by) % 4) * 8 + y * 2 + core
+
+    def along_y(by):
+        return x * 8 + ((y + by) % 4) * 2 + core
+
+    firsts = [(z, jnp.where(even, along_x(by), along_y(by))) for by in (1, 2, 3)]
+    seconds = [(z, jnp.where(even, along_y(by), along_x(by))) for by in (1, 2, 3)]
 
     def rows32(b):
         return pl.ds(pl.multiple_of(((b + 4) % 4) * 32, 32), 32)
 
-    def cols(b):
-        return pl.ds(pl.multiple_of(((b + 4) % 4) * 128, 128), 128)
-
-    def spot(a):
-        first = a % 2
-        return first, 1 - first, jnp.where(first == 0, x, y), jnp.where(first == 0, y, x)
-
-    def copies(a, n):
-        first, second, u, v = spot(a)
+    def members(g):
+        return pl.ds(g * GROUP, GROUP)
+
+    def copies(g, n, landing):
         made = []
-        for by in (1, 2, 3):
+        for k in range(3):
+            by = k + 1
             if n == 0:
-                src, dst = cur_ref.at[a, rows32(u + by)], a_ref.at[a, by - 1]
+                src, dst = cur_ref.at[members(g), rows32(u + by)], a_ref.at[g, k]
+                if landing:
+                    src = dst
             elif n == 1:
-                src, dst = cur_ref.at[a, rows32(u), cols(v + by)], b_ref.at[a, by - 1]
-            elif n == 2:
-                src = dst = blk_ref.at[a, :, cols(v)]
+                src = dst = b_ref.at[g, (v - by + 4) % 4 if landing else v]
             else:
-                src = dst = out_ref.at[core, a, rows32(u)]
-            axis = first if n in (0, 3) else second
-            sem = (a, n, by - 1)
-            made.append(remote(src, dst, send_sem.at[sem], recv_sem.at[sem], near(axis, by)))
+                src = dst = out_ref.at[core, members(g), rows32(u - by if landing else u)]
+            device = seconds[k] if n == 1 else firsts[k]
+            made.append(remote(src, dst, send_sem.at[g, n, k], recv_sem.at[g, n, k], device))
         return made
 
-    def start(a, n):
-        for copy in copies(a, n):
+    def start(g, n):
+        for copy in copies(g, n, False):
             copy.start()
 
-    def arrive(a, n):
-        first, second, u, v = spot(a)
-        for by in (1, 2, 3):
-            if n == 0:
-                dst = a_ref.at[a, by - 1]
-            elif n == 1:
-                dst = b_ref.at[a, by - 1]
-            elif n == 2:
-                dst = blk_ref.at[a, :, cols(v - by)]
-            else:
-                dst = out_ref.at[core, a, rows32(u - by)]
-            axis = first if n in (0, 3) else second
-            sem = (a, n, by - 1)
-            remote(dst, dst, send_sem.at[sem], recv_sem.at[sem], near(axis, by)).wait_recv()
-
-    def pair_copy(a):
-        return remote(send_ref.at[a], got_ref.at[a], pair_send.at[0, a], pair_recv.at[0, a], sibling)
-
-    def give_copy(a, which):
-        here = out_ref.at[which, a]
-        return remote(here, here, pair_send.at[1, a], pair_recv.at[1, a], sibling)
-
-    def loads(a):
+    def arrive(g, n):
+        for copy in copies(g, n, True):
+            copy.wait_recv()
+
+    def pair_copy(g):
+        rows = members(g)
+        return remote(send_ref.at[rows], got_ref.at[rows], pair_send.at[0, g], pair_recv.at[0, g], sibling)
+
+    def give_copy(g, which):
+        here = out_ref.at[which, members(g)]
+        return remote(here, here, pair_send.at[1, g], pair_recv.at[1, g], sibling)
+
+    def loads(g):
+        rows = members(g)
         return [
-            pltpu.make_async_copy(left_hbm.at[a], left_ref.at[a], load_sem.at[0, a]),
-            pltpu.make_async_copy(right_hbm.at[a], right_ref.at[a], load_sem.at[1, a]),
-            pltpu.make_async_copy(probe_hbm.at[a], probe_ref.at[a], load_sem.at[2, a]),
+            pltpu.make_async_copy(left_hbm.at[rows], left_ref.at[rows], load_sem.at[0, g]),
+            pltpu.make_async_copy(right_hbm.at[rows], right_ref.at[rows], load_sem.at[1, g]),
+            pltpu.make_async_copy(probe_hbm.at[rows], probe_ref.at[rows], load_sem.at[2, g]),
         ]
 
-    def compute(a):
+    def compute(g):
         column = step_ref[0]
-        for copy in loads(a):
+        for copy in loads(g):
             copy.wait()
         level = lax.broadcasted_iota(jnp.int32, (128, 96), 1)
-        live = z * 6 + a > column
-        range_sum = jnp.zeros((128, 512), F32)
-        co_sum = jnp.zeros((128, 512), F32)
-        for j in range(3):
-            tile = c * 3 + j
-            own = tile == column
-            depth = jnp.where(live & (tile <= column), ranks_ref[j, a], 0)
-            keep = level < depth
-            left = left_ref[a, j]
-            right = right_ref[a, j]
-            both = dot_nt(stack_ref[j], right)
-            coupled = both[:96].astype(BF16)
-            mixed = dot_nn(reduced_ref[j], coupled)
-            mixed = jnp.where(own, -both[96:], mixed)
-            mixed = jnp.where(keep, mixed, 0.0).astype(BF16)
-            probed = dot_nt(probe_ref[a], left)
-            probed = jnp.where(keep, probed, 0.0).astype(BF16)
-            folded = dot_nt(probed, coupled).astype(BF16)
-            folded = jnp.where(own, -probed, folded)
-            closing = jnp.where(own, right, upper_ref[j, 1])
-            range_sum += dot_nn(mixed, left)
-            co_sum += dot_nn(folded, closing)
-        even = core == 0
-        acc_ref[a] = -jnp.where(even, range_sum, co_sum)
-        send_ref[a] = -jnp.where(even, co_sum, range_sum).astype(BF16)
-        pair_copy(a).start()
-
-    def stage(n, a):
-        first, second, u, v = spot(a)
+        tiles = [c * 3 + j for j in range(3)]
+        both = [
+            dot_nt(right_ref[members(g), j].reshape(GROUP * 96, 512), stack_ref[j]) for j in range(3)
+        ]
+        for k in range(GROUP):
+            a = g * GROUP + k
+            part = slice(96 * k, 96 * (k + 1))
+            live = z * 6 + a > column
+            own_reduced = jnp.where(
+                tiles[0] == column,
+                both[0][part, :128],
+                jnp.where(tiles[1] == column, both[1][part, :128], both[2][part, :128]),
+            )
+            own_mixed = -own_reduced.T
+            range_sum = jnp.zeros((128, 512), F32)
+            co_sum = jnp.zeros((128, 512), F32)
+            for j in range(3):
+                own = tiles[j] == column
+                depth = jnp.where(live & (tiles[j] <= column), ranks_ref[j, a], 0)
+                keep = level < depth
+                left = left_ref[a, j]
+                coupled = both[j][part, 128:].astype(BF16)
+                mixed = jnp.where(own, own_mixed, dot_nt(reduced_ref[j], coupled))
+                mixed = jnp.where(keep, mixed, 0.0).astype(BF16)
+                probed = dot_nt(probe_ref[a], left)
+                probed = jnp.where(keep, probed, 0.0).astype(BF16)
+                folded = dot_nn(probed, coupled).astype(BF16)
+                folded = jnp.where(own, -probed, folded)
+                closing = jnp.where(own, right_ref[a, j], upper_ref[j, 1])
+                range_sum += dot_nn(mixed, left)
+                co_sum += dot_nn(folded, closing)
+            acc_ref[a] = -jnp.where(even, range_sum, co_sum)
+            send_ref[a] = -jnp.where(even, co_sum, range_sum).astype(BF16)
+        pair_copy(g).start()
+
+    def stage(n, g):
+        rows = members(g)
         if n == 0:
-            pair_copy(a).wait_recv()
+            pair_copy(g).wait_recv()
             for by in range(4):
-                rows = rows32(u + by)
-                total = acc_ref[a, rows] + got_ref[a, rows].astype(F32)
+                block = rows32(u + by)
+                total = acc_ref[rows, block] + got_ref[rows, block].astype(F32)
                 if by:
-                    cur_ref[a, rows] = total.astype(BF16)
+                    cur_ref[rows, block] = total.astype(BF16)
                 else:
-                    acc_ref[a, rows] = total
-            start(a, 0)
+                    acc_ref[rows, block] = total
+            start(g, 0)
         elif n == 1:
-            arrive(a, 0)
-            rows = rows32(u)
-            total = acc_ref[a, rows]
-            for d in range(3):
-                total += a_ref[a, d].astype(F32)
-            acc_ref[a, rows] = total
-            cur_ref[a, rows] = total.astype(BF16)
-            start(a, 1)
+            arrive(g, 0)
+            total = acc_ref[rows, rows32(u)]
+            for k in range(3):
+                total += a_ref[g, k].astype(F32)
+            b_ref[g, v] = total.astype(BF16)
+            start(g, 1)
         elif n == 2:
-            arrive(a, 1)
-            total = acc_ref[a, rows32(u), cols(v)]
-            for d in range(3):
-                total += b_ref[a, d].astype(F32)
-            blk_ref[a, :, cols(v)] = total.astype(BF16)
-            start(a, 2)
+            arrive(g, 1)
+            total = b_ref[g, 0].astype(F32)
+            for b in range(1, 4):
+                total += b_ref[g, b].astype(F32)
+            block = total.astype(BF16)
+
+            @pl.when(even)
+            def _():
+                out_ref[0, rows, rows32(u)] = block
+
+            @pl.when(jnp.logical_not(even))
+            def _():
+                solved = dot_nn(block.reshape(GROUP * 32, 512), solve_ref[...]).astype(BF16)
+                out_ref[1, rows, rows32(u)] = solved.reshape(GROUP, 32, 512)
+
+            start(g, 2)
         elif n == 3:
-            arrive(a, 2)
-
-            @pl.when(core == 0)
-            def _():
-                out_ref[0, a, rows32(u)] = blk_ref[a]
-
-            @pl.when(core == 1)
-            def _():
-                out_ref[1, a, rows32(u)] = dot_nn(blk_ref[a], solve_ref[...]).astype(BF16)
-
-            start(a, 3)
-        elif n == 4:
-            arrive(a, 3)
-            give_copy(a, core).start()
+            arrive(g, 2)
+            give_copy(g, core).start()
         else:
-            give_copy(a, 1 - core).wait_recv()
+            give_copy(g, 1 - core).wait_recv()
 
     @pl.when(z < FIRST)
     def _():
@@ -472,46 +473,45 @@
 
     @pl.when(z >= FIRST)
     def _():
-        for a in range(6):
-            for copy in loads(a):
+        for g in range(GROUPS):
+            for copy in loads(g):
                 copy.start()
         barrier = pltpu.get_barrier_semaphore()
-        peers = (sibling, near(0, 1), near(0, 2), near(0, 3), near(1, 1), near(1, 2), near(1, 3))
-        for device in peers:
+        for device in (sibling, *firsts, *seconds):
             pl.semaphore_signal(barrier, inc=1, device_id=device, device_id_type=MESH)
         flat = sketch_ref[...].astype(F32).T.astype(BF16)
         for j in range(3):
-            stack_ref[j, :96] = upper_ref[j, 0]
-            stack_ref[j, 96:] = flat
+            stack_ref[j, :128] = flat
+            stack_ref[j, 128:] = upper_ref[j, 0]
             reduced = dot_nn(upper_ref[j, 1], sketch_ref[...]).astype(BF16).astype(F32)
             reduced_ref[j] = reduced.T.astype(BF16)
         pl.semaphore_wait(barrier, 7)
 
         def slot(t, _):
-            @pl.when(t < 6)
+            @pl.when(t < GROUPS)
             def _():
                 compute(t)
 
-            for n in reversed(range(6)):
-                a = t - 1 - n
-
-                @pl.when((a >= 0) & (a < 6))
-                def _(n=n, a=a):
-                    stage(n, a)
+            for n in reversed(range(5)):
+                g = t - 1 - n
+
+                @pl.when((g >= 0) & (g < GROUPS))
+                def _(n=n, g=g):
+                    stage(n, g)
 
             return 0
 
-        lax.fori_loop(0, 12, slot, 0)
-
-        def finish(a, _):
-            pair_copy(a).wait_send()
-            give_copy(a, core).wait_send()
-            for n in range(4):
-                for copy in copies(a, n):
+        lax.fori_loop(0, GROUPS + 5, slot, 0)
+
+        def finish(g, _):
+            pair_copy(g).wait_send()
+            give_copy(g, core).wait_send()
+            for n in range(3):
+                for copy in copies(g, n, False):
                     copy.wait_send()
             return 0
 
-        lax.fori_loop(0, 6, finish, 0)
+        lax.fori_loop(0, GROUPS, finish, 0)
 
 
 def row_sums(ranks, step, left, right, probes, upper, sketch, solve):
@@ -533,14 +533,13 @@
             pltpu.VMEM((6, 128, 512), BF16),
             pltpu.VMEM((6, 128, 512), F32),
             pltpu.VMEM((6, 128, 512), BF16),
-            pltpu.VMEM((6, 3, 32, 512), BF16),
-            pltpu.VMEM((6, 3, 32, 128), BF16),
-            pltpu.VMEM((6, 32, 512), BF16),
-            pltpu.SemaphoreType.DMA((3, 6)),
-            pltpu.SemaphoreType.DMA((6, 4, 3)),
-            pltpu.SemaphoreType.DMA((6, 4, 3)),
-            pltpu.SemaphoreType.DMA((2, 6)),
-            pltpu.SemaphoreType.DMA((2, 6)),
+            pltpu.VMEM((GROUPS, 3, GROUP, 32, 512), BF16),
+            pltpu.VMEM((GROUPS, 4, GROUP, 32, 512), BF16),
+            pltpu.SemaphoreType.DMA((3, GROUPS)),
+            pltpu.SemaphoreType.DMA((GROUPS, 3, 3)),
+            pltpu.SemaphoreType.DMA((GROUPS, 3, 3)),
+            pltpu.SemaphoreType.DMA((2, GROUPS)),
+            pltpu.SemaphoreType.DMA((2, GROUPS)),
         ],
         compiler_params=pltpu.CompilerParams(
             collective_id=0, has_side_effects=True, vmem_limit_bytes=50 * 2**20

time: 90.3 us -> 78.7 us (0.87)
  Pallas kernels: 86.2 us -> 74.8 us
    pallas_call x1, Pallas kernels: 59.5 us -> 47.5 us  [row_sums(): pl.pallas_call(row_kernel, out_shape=jax.ShapeDtypeStruct((2, 6, 128, 512...]
where the time goes in v3:
time: 78.7 us; the launch traced here: 77.5 us
  Pallas kernels  74.8 us (95%)
  between operations  1.37 us (2%)
  local copies, waits for them, and re-layouts  1.27 us (2%)
    pallas_call x1, Pallas kernels, row_sums(): pl.pallas_call(row_kernel, out_shape=jax.ShapeDtypeStruct((2, 6, 128, 512...  47.5 us
    pallas_call x1, Pallas kernels, spread_panel(): pl.pallas_call(functools.partial(panel_kernel, owner), out_shape=jax.Shap...  26.6 us

profile of v3, /device:TPU:481, one launch (start us, length us, event | category | flops | bytes accessed | tf_op | source)
XLA Modules:
  0.0 77.5 jit_solution(14749508755252120339)
XLA Ops:
  1.3 0.7 gather_panel.1
  2.0 0.0 copy-start
  2.0 0.0 copy-start.1
  2.0 0.0 copy-start.2
  2.1 0.0 copy-start.3
  2.1 26.7 %conditional.1 = (bf16[3,2,96,512]{3,2,1,0:T(8,128)(2,1)S(1)}) conditional(s32[]{:T(128)} %bitcast.1, bf16[6,2,96,512]{3,2,1,0:T(8,128)(2,1)S(1)} %gather_panel.1, bf16[6,2,96,512]{3,2,1,0:T(8,128)(2,1)S(1)} %gather_panel.1, bf16[6,2,96,512]{3,2,1,0:T(8,128)(2,1)S(1)} %gather_panel.1, ...), branch_computations={%region_0.0_spmd, %region_1.0_spmd, %region_2.0_spmd, %region_3.0_... | conditional | bytes 8 | solution.py:555
  2.1 26.6 %spread_panel.22 = bf16[3,2,96,512]{3,2,1,0:T(8,128)(2,1)S(1)} custom-call(bf16[6,2,96,512]{3,2,1,0:T(8,128)(2,1)S(1)} %panel_ref.6), custom_call_target="tpu_custom_call" | custom-call | tf_op jit(solution)/shard_map/cond/branch_6_fun/spread_panel/pallas_call | solution.py:281
  28.7 0.0 copy-done
  28.7 0.0 copy-done.1
  28.7 0.0 copy-done.2
  28.8 0.0 copy-done.3
  28.8 47.5 %row_sums.1 = bf16[2,6,128,512]{3,2,1,0:T(8,128)(2,1)S(1)} custom-call(s32[3,6]{1,0:T(4,128)S(1)} %bitcast.7, s32[1]{0:T(128)S(6)} %copy.25.step_ref, bf16[6,3,96,512]{3,2,1,0:T(8,128)(2,1)} %left_hbm.1, bf16[6,3,96,512]{3,2,1,0:T(8,128)(2,1)} %right_hbm.1, bf16[6,128,512]{2,1,0:T(8,128)(2,1)S(1)} %copy-done, ...), custom_call_target="tpu_custom_call" | custom-call | tf_op jit(solution)/shard_map/row_sums/pallas_call | solution.py:521
  76.3 1.2 %slice_bitcast_fusion = (bf16[6,128,512]{2,1,0:T(8,128)(2,1)}, bf16[6,128,512]{2,1,0:T(8,128)(2,1)}) fusion(bf16[2,6,128,512]{3,2,1,0:T(8,128)(2,1)S(1)} %row_sums.1), kind=kLoop, calls=%fused_computation | loop fusion | bytes 3145728 | tf_op jit(solution)/shard_map/squeeze | solution.py:559
Async XLA Ops:
  2.0 26.7 %copy-start = (bf16[6,128,512]{2,1,0:T(8,128)(2,1)S(1)}, bf16[6,128,512]{2,1,0:T(8,128)(2,1)}, u32[]{:S(2)}) copy-start(bf16[6,128,512]{2,1,0:T(8,128)(2,1)} %probe_hbm.1) | copy-start | bytes 2359300
  2.0 26.7 %copy-start.1 = (bf16[512,512]{1,0:T(8,128)(2,1)S(1)}, bf16[512,512]{1,0:T(8,128)(2,1)}, u32[]{:S(2)}) copy-start(bf16[512,512]{1,0:T(8,128)(2,1)} %solve_ref.1) | copy-start | bytes 1572868
  2.0 26.7 %copy-start.2 = (bf16[512,128]{1,0:T(8,128)(2,1)S(1)}, bf16[512,128]{1,0:T(8,128)(2,1)}, u32[]{:S(2)}) copy-start(bf16[512,128]{1,0:T(8,128)(2,1)} %sketch_ref.1) | copy-start | bytes 393220
  2.1 26.7 %copy-start.3 = (s32[6,3]{0,1:T(4,128)S(1)}, s32[6,3]{0,1:T(4,128)}, u32[]{:S(2)}) copy-start(s32[6,3]{0,1:T(4,128)} %param.25) | copy-start | bytes 220

commit v4 on v3

v4 whole, which is shorter than its diff:
```python
import functools

import jax
import jax.numpy as jnp
from jax import lax
from jax.experimental import pallas as pl
from jax.experimental.pallas import tpu as pltpu
from jax.sharding import PartitionSpec as P

MESH = pl.DeviceIdType.MESH
F32 = jnp.float32
BF16 = jnp.bfloat16
FIRST = 8
LAST = 15
HALF = 48
CHUNKS = 12


def remote(src, dst, send_sem, recv_sem, device):
    return pltpu.make_async_remote_copy(
        src_ref=src,
        dst_ref=dst,
        send_sem=send_sem,
        recv_sem=recv_sem,
        device_id=device,
        device_id_type=MESH,
    )


def line_trees():
    trees = []
    for s in range(16):
        parent = {}

        def chain(*planes):
            for before, after in zip(planes, planes[1:]):
                parent[after] = before

        low = s < FIRST
        if low or s == 15:
            chain(*((s, 4, 9) if s < 2 else (s, 5, 9) if s == 15 else (s, 9)), 10, 11)
            chain(9, 8)
        if low or s == 8:
            chain(*((s, 3, 14) if 6 <= s < 8 else (s, 2, 14) if s == 8 else (s, 14)), 13, 12)
            chain(14, 15)
        if s == 8:
            chain(8, 9, 10, 11)
        if s == 15:
            chain(15, 14, 13, 12)
        if s == 9:
            chain(9, 10, 11, 12, 13)
            chain(9, 8, 2, 15, 14)
        if s == 14:
            chain(14, 13, 12, 11, 10)
            chain(14, 15, 5, 8, 9)
        if 10 <= s <= 13:
            chain(*range(s, 16))
            chain(*range(s, 7, -1))
        trees.append(parent)
    return trees


def table_words(entries):
    return [
        sum(entries[s][4 * w + d] * 16**d for d in range(4)) for s in range(16) for w in range(4)
    ]


def tree_tables():
    none = [list(range(16)) for _ in range(16)]
    parents = [list(row) for row in none]
    firsts = [list(row) for row in none]
    seconds = [list(row) for row in none]
    for s, tree in enumerate(line_trees()):
        for plane, before in tree.items():
            parents[s][plane] = before
            if firsts[s][before] == before:
                firsts[s][before] = plane
            else:
                assert seconds[s][before] == before
                seconds[s][before] = plane
    return [table_words(entries) for entries in (parents, firsts, seconds)]


def look_up(words, s, z):
    index = s * 4 + z // 4
    word = words[0]
    for k, value in enumerate(words):
        if k:
            word = jnp.where(index == k, value, word)
    digit = z % 4
    scale = jnp.where(digit == 0, 1, jnp.where(digit == 1, 16, jnp.where(digit == 2, 256, 4096)))
    return (word // scale) % 16


def gather_kernel(ranks_ref, step_ref, left_ref, right_ref, panel_ref, sems):
    column = step_ref[0]
    slot = lax.rem(column, 3)

    @pl.when(lax.axis_index("col") == column // 3)
    def _():
        copies = [
            pltpu.make_async_copy(left_ref.at[:, slot], panel_ref.at[:, 0], sems.at[0]),
            pltpu.make_async_copy(right_ref.at[:, slot], panel_ref.at[:, 1], sems.at[1]),
        ]
        for copy in copies:
            copy.start()
        for copy in copies:
            copy.wait()
        level = lax.broadcasted_iota(jnp.int32, (96, 512), 0)
        for i in range(6):
            tile = panel_ref[i, 0]
            panel_ref[i, 0] = jnp.where(level < ranks_ref[slot, i], tile, jnp.zeros_like(tile))


def gather_panel(ranks, step, left, right):
    return pl.pallas_call(
        gather_kernel,
        out_shape=jax.ShapeDtypeStruct((6, 2, 96, 512), BF16),
        in_specs=[
            pl.BlockSpec(memory_space=pltpu.SMEM),
            pl.BlockSpec(memory_space=pltpu.SMEM),
            pl.BlockSpec(memory_space=pl.ANY),
            pl.BlockSpec(memory_space=pl.ANY),
        ],
        out_specs=pl.BlockSpec(memory_space=pltpu.VMEM),
        scratch_shapes=[pltpu.SemaphoreType.DMA((2,))],
        compiler_params=pltpu.CompilerParams(vmem_limit_bytes=62 * 2**20),
        name="gather_panel",
    )(ranks, step, left, right)


def home_kernel(owner, panel_ref, out_ref, send_sem, recv_sem, local_sem):
    z = lax.axis_index("row")
    c = lax.axis_index("col")
    owner_line = owner // 2
    owner_core = owner % 2
    is_owner = c == owner
    is_home = (c // 2 == z) & jnp.logical_not(is_owner)
    holds_own = is_owner & (z == owner_line)
    barrier = pltpu.get_barrier_semaphore()

    @pl.when(is_home)
    def _():
        pl.semaphore_signal(barrier, inc=1, device_id=(z, owner), device_id_type=MESH)

    def copy(core):
        part = panel_ref.at[pl.ds(3 * core, 3)]
        return remote(part, out_ref, send_sem.at[core], recv_sem, (z, 2 * z + core))

    @pl.when(is_owner)
    def _():
        pl.semaphore_wait(barrier, jnp.where(z == owner_line, 1, 2))

    for core in range(2):
        flag = is_owner if core != owner_core else is_owner & (z != owner_line)

        @pl.when(flag)
        def _(core=core):
            copy(core).start()

    @pl.when(holds_own)
    def _():
        own = pltpu.make_async_copy(panel_ref.at[pl.ds(3 * owner_core, 3)], out_ref, local_sem)
        own.start()
        own.wait()

    @pl.when(is_home)
    def _():
        remote(out_ref, out_ref, send_sem.at[0], recv_sem, (z, owner)).wait_recv()

    for core in range(2):
        flag = is_owner if core != owner_core else is_owner & (z != owner_line)

        @pl.when(flag)
        def _(core=core):
            copy(core).wait_send()


def send_home(owner, panel):
    return pl.pallas_call(
        functools.partial(home_kernel, owner),
        out_shape=jax.ShapeDtypeStruct((3, 2, 96, 512), BF16),
        in_specs=[pl.BlockSpec(memory_space=pltpu.VMEM)],
        out_specs=pl.BlockSpec(memory_space=pltpu.VMEM),
        scratch_shapes=[
            pltpu.SemaphoreType.DMA((2,)),
            pltpu.SemaphoreType.DMA,
            pltpu.SemaphoreType.DMA,
        ],
        compiler_params=pltpu.CompilerParams(
            collective_id=owner - 15, has_side_effects=True, vmem_limit_bytes=16 * 2**20
        ),
        name="send_home",
    )(panel)


def dot_nt(a, b):
    return lax.dot_general(a, b, (((1,), (1,)), ((), ())), preferred_element_type=F32)


def dot_nn(a, b):
    return jnp.dot(a, b, preferred_element_type=F32)


GROUP = 2
GROUPS = 6 // GROUP


def row_kernel(
    ranks_ref, step_ref, left_hbm, right_hbm, probe_hbm, home_ref, sketch_ref, solve_ref, out_ref,
    upper_ref, left_ref, right_ref, probe_ref, probed_ref, stack_ref, reduced_ref,
    range_ref, co_ref, send_ref, got_ref, acc_ref, cur_ref, a_ref, b_ref,
    home_sem, up_send, down_send, chunk_sem, load_sem, send_sem, recv_sem, pair_send, pair_recv,
):
    z = lax.axis_index("row")
    c = lax.axis_index("col")
    x = c // 8
    y = (c // 2) % 4
    core = c % 2
    even = core == 0
    sibling = (z, c + 1 - 2 * core)
    u = jnp.where(even, x, y)
    v = jnp.where(even, y, x)

    def along_x(by):
        return ((x + by) % 4) * 8 + y * 2 + core

    def along_y(by):
        return x * 8 + ((y + by) % 4) * 2 + core

    firsts = [(z, jnp.where(even, along_x(by), along_y(by))) for by in (1, 2, 3)]
    seconds = [(z, jnp.where(even, along_y(by), along_x(by))) for by in (1, 2, 3)]

    def rows32(b):
        return pl.ds(pl.multiple_of(((b + 4) % 4) * 32, 32), 32)

    def members(g):
        return pl.ds(g * GROUP, GROUP)

    def copies(g, n, landing):
        made = []
        for k in range(3):
            by = k + 1
            if n == 0:
                src, dst = cur_ref.at[members(g), rows32(u + by)], a_ref.at[g, k]
                if landing:
                    src = dst
            elif n == 1:
                src = dst = b_ref.at[g, (v - by + 4) % 4 if landing else v]
            else:
                src = dst = out_ref.at[core, members(g), rows32(u - by if landing else u)]
            device = seconds[k] if n == 1 else firsts[k]
            made.append(remote(src, dst, send_sem.at[g, n, k], recv_sem.at[g, n, k], device))
        return made

    def start(g, n):
        for copy in copies(g, n, False):
            copy.start()

    def arrive(g, n):
        for copy in copies(g, n, True):
            copy.wait_recv()

    def pair_copy(g):
        rows = members(g)
        return remote(send_ref.at[rows], got_ref.at[rows], pair_send.at[0, g], pair_recv.at[0, g], sibling)

    def give_copy(g, which):
        here = out_ref.at[which, members(g)]
        return remote(here, here, pair_send.at[1, g], pair_recv.at[1, g], sibling)

    def loads(g):
        rows = members(g)
        return [
            pltpu.make_async_copy(left_hbm.at[rows], left_ref.at[rows], load_sem.at[0, g]),
            pltpu.make_async_copy(right_hbm.at[rows], right_ref.at[rows], load_sem.at[1, g]),
            pltpu.make_async_copy(probe_hbm.at[rows], probe_ref.at[rows], load_sem.at[2, g]),
        ]

    line = c // 2
    home = z == line
    target = z >= FIRST
    parent, first, second = (look_up(words, line, z) for words in tree_tables())
    receives = parent != z
    up = first != z
    down = second != z

    def piece(q):
        return q // 4, (q // 2) % 2, pl.ds(pl.multiple_of((q % 2) * HALF, HALF), HALF)

    def chunk_copy(ref, sems, plane, q):
        t, side, rows = piece(q)
        return remote(
            ref.at[t, side, rows], upper_ref.at[t, side, rows], sems.at[q], chunk_sem.at[q], (plane, c)
        )

    def forward(ref, q):
        @pl.when(up)
        def _():
            chunk_copy(ref, up_send, first, q).start()

        @pl.when(down)
        def _():
            chunk_copy(ref, down_send, second, q).start()

    def relay(q):
        @pl.when(receives)
        def _():
            chunk_copy(upper_ref, up_send, parent, q).wait_recv()
            forward(upper_ref, q)

    def keep_of(a, t):
        tile = c * 3 + t
        live = z * 6 + a > step_ref[0]
        depth = jnp.where(live & (tile <= step_ref[0]), ranks_ref[t, a], 0)
        return lax.broadcasted_iota(jnp.int32, (128, 96), 1) < depth

    def probes(g, _):
        for copy in loads(g):
            copy.wait()
        for k in range(GROUP):
            a = g * GROUP + k
            range_ref[a] = jnp.zeros((128, 512), F32)
            co_ref[a] = jnp.zeros((128, 512), F32)
            for t in range(3):
                probed = dot_nt(probe_ref[a], left_ref[a, t])
                probed_ref[a, t] = jnp.where(keep_of(a, t), probed, 0.0).astype(BF16)
        return 0

    def open_tile(t):
        stack_ref[128:] = upper_ref[t, 0]
        reduced = dot_nn(upper_ref[t, 1], sketch_ref[...]).astype(BF16).astype(F32)
        reduced_ref[...] = reduced.T.astype(BF16)

    def compute(t, g):
        own = c * 3 + t == step_ref[0]
        both = dot_nt(right_ref[members(g), t].reshape(GROUP * 96, 512), stack_ref[...])
        for k in range(GROUP):
            a = g * GROUP + k
            part = slice(96 * k, 96 * (k + 1))
            coupled = both[part, 128:].astype(BF16)
            mixed = jnp.where(own, -both[part, :128].T, dot_nt(reduced_ref[...], coupled))
            mixed = jnp.where(keep_of(a, t), mixed, 0.0).astype(BF16)
            probed = probed_ref[a, t]
            folded = jnp.where(own, -probed, dot_nn(probed, coupled).astype(BF16))
            closing = jnp.where(own, right_ref[a, t], upper_ref[t, 1])
            range_ref[a] += dot_nn(mixed, left_ref[a, t])
            co_ref[a] += dot_nn(folded, closing)

            @pl.when((t < 2) & (g < 2))
            def _(k=k):
                relay(t * 4 + 4 + g * 2 + k)

    def close_rows(g):
        for k in range(GROUP):
            a = g * GROUP + k
            acc_ref[a] = -jnp.where(even, range_ref[a], co_ref[a])
            send_ref[a] = -jnp.where(even, co_ref[a], range_ref[a]).astype(BF16)
        pair_copy(g).start()

    def stage(n, g):
        rows = members(g)
        if n == 0:
            pair_copy(g).wait_recv()
            for by in range(4):
                block = rows32(u + by)
                total = acc_ref[rows, block] + got_ref[rows, block].astype(F32)
                if by:
                    cur_ref[rows, block] = total.astype(BF16)
                else:
                    acc_ref[rows, block] = total
            start(g, 0)
        elif n == 1:
            arrive(g, 0)
            total = acc_ref[rows, rows32(u)]
            for k in range(3):
                total += a_ref[g, k].astype(F32)
            b_ref[g, v] = total.astype(BF16)
            start(g, 1)
        elif n == 2:
            arrive(g, 1)
            total = b_ref[g, 0].astype(F32)
            for b in range(1, 4):
                total += b_ref[g, b].astype(F32)
            block = total.astype(BF16)

            @pl.when(even)
            def _():
                out_ref[0, rows, rows32(u)] = block

            @pl.when(jnp.logical_not(even))
            def _():
                solved = dot_nn(block.reshape(GROUP * 32, 512), solve_ref[...]).astype(BF16)
                out_ref[1, rows, rows32(u)] = solved.reshape(GROUP, 32, 512)

            start(g, 2)
        elif n == 3:
            arrive(g, 2)
            give_copy(g, core).start()
        else:
            give_copy(g, 1 - core).wait_recv()

    @pl.when(target)
    def _():
        for g in range(GROUPS):
            for copy in loads(g):
                copy.start()

    barrier = pltpu.get_barrier_semaphore()

    @pl.when(receives)
    def _():
        pl.semaphore_signal(barrier, inc=1, device_id=(parent, c), device_id_type=MESH)

    @pl.when(target)
    def _():
        for device in (sibling, *firsts, *seconds):
            pl.semaphore_signal(barrier, inc=1, device_id=device, device_id_type=MESH)

    peers = jnp.where(up, 1, 0) + jnp.where(down, 1, 0) + jnp.where(target, 7, 0)

    @pl.when(peers > 0)
    def _():
        pl.semaphore_wait(barrier, peers)

    @pl.when(home)
    def _():
        own = pltpu.make_async_copy(home_ref, upper_ref, home_sem)
        own.start()
        lax.fori_loop(0, CHUNKS, lambda q, _: (forward(home_ref, q), 0)[1], 0)
        own.wait()

    @pl.when(jnp.logical_not(target))
    def _():
        out_ref[...] = jnp.zeros_like(out_ref)
        lax.fori_loop(0, CHUNKS, lambda q, _: (relay(q), 0)[1], 0)

    @pl.when(target)
    def _():
        stack_ref[:128] = sketch_ref[...].astype(F32).T.astype(BF16)
        lax.fori_loop(0, GROUPS, probes, 0)
        lax.fori_loop(0, 4, lambda q, _: (relay(q), 0)[1], 0)

        def step(i, _):
            t = i // GROUPS
            g = i % GROUPS

            @pl.when(t < 3)
            def _():
                @pl.when(g == 0)
                def _():
                    open_tile(t)

                compute(t, g)

            @pl.when(t == 2)
            def _():
                close_rows(g)

            for n in reversed(range(5)):
                late = i - 2 * GROUPS - 1 - n

                @pl.when((late >= 0) & (late < GROUPS))
                def _(n=n, late=late):
                    stage(n, late)

            return 0

        lax.fori_loop(0, 3 * GROUPS + 5, step, 0)

        def finish(g, _):
            pair_copy(g).wait_send()
            give_copy(g, core).wait_send()
            for n in range(3):
                for copy in copies(g, n, False):
                    copy.wait_send()
            return 0

        lax.fori_loop(0, GROUPS, finish, 0)

    @pl.when(up)
    def _():
        lax.fori_loop(
            0, CHUNKS, lambda q, _: (chunk_copy(upper_ref, up_send, first, q).wait_send(), 0)[1], 0
        )

    @pl.when(down)
    def _():
        lax.fori_loop(
            0, CHUNKS, lambda q, _: (chunk_copy(upper_ref, down_send, second, q).wait_send(), 0)[1], 0
        )


def row_sums(ranks, step, left, right, probes, home, sketch, solve):
    vmem = pl.BlockSpec(memory_space=pltpu.VMEM)
    smem = pl.BlockSpec(memory_space=pltpu.SMEM)
    hbm = pl.BlockSpec(memory_space=pl.ANY)
    return pl.pallas_call(
        row_kernel,
        out_shape=jax.ShapeDtypeStruct((2, 6, 128, 512), BF16),
        in_specs=[smem, smem, hbm, hbm, hbm, vmem, vmem, vmem],
        out_specs=vmem,
        scratch_shapes=[
            pltpu.VMEM((3, 2, 96, 512), BF16),
            pltpu.VMEM((6, 3, 96, 512), BF16),
            pltpu.VMEM((6, 3, 96, 512), BF16),
            pltpu.VMEM((6, 128, 512), BF16),
            pltpu.VMEM((6, 3, 128, 96), BF16),
            pltpu.VMEM((224, 512), BF16),
            pltpu.VMEM((128, 96), BF16),
            pltpu.VMEM((6, 128, 512), F32),
            pltpu.VMEM((6, 128, 512), F32),
            pltpu.VMEM((6, 128, 512), BF16),
            pltpu.VMEM((6, 128, 512), BF16),
            pltpu.VMEM((6, 128, 512), F32),
            pltpu.VMEM((6, 128, 512), BF16),
            pltpu.VMEM((GROUPS, 3, GROUP, 32, 512), BF16),
            pltpu.VMEM((GROUPS, 4, GROUP, 32, 512), BF16),
            pltpu.SemaphoreType.DMA,
            pltpu.SemaphoreType.DMA((CHUNKS,)),
            pltpu.SemaphoreType.DMA((CHUNKS,)),
            pltpu.SemaphoreType.DMA((CHUNKS,)),
            pltpu.SemaphoreType.DMA((3, GROUPS)),
            pltpu.SemaphoreType.DMA((GROUPS, 3, 3)),
            pltpu.SemaphoreType.DMA((GROUPS, 3, 3)),
            pltpu.SemaphoreType.DMA((2, GROUPS)),
            pltpu.SemaphoreType.DMA((2, GROUPS)),
        ],
        compiler_params=pltpu.CompilerParams(
            collective_id=0, has_side_effects=True, vmem_limit_bytes=50 * 2**20
        ),
        name="row_sums",
    )(ranks, step, left, right, probes, home, sketch, solve)


def body(left_factors, right_factors, ranks, sketch_left, sketch_right, upper_inverse, step):
    slots = ranks.T
    panel = gather_panel(slots, step, left_factors, right_factors)
    branches = [functools.partial(send_home, owner) for owner in range(16, 32)]
    home = lax.switch(lax.div(step[0], 3) - 16, branches, panel)
    out = row_sums(
        slots, step, left_factors, right_factors, sketch_left, home, sketch_right, upper_inverse
    )
    return (out[0], out[1])


def solution(mesh):
    return jax.shard_map(
        body,
        mesh=mesh,
        in_specs=(
            P("row", "col", None, None),
            P("row", "col", None, None),
            P("row", "col"),
            P("row", None, None),
            P(),
            P(),
            P(),
        ),
        out_specs=(P("row", None, None), P("row", None, None)),
        check_vma=False,
    )
```

time: 78.7 us -> 87.7 us (1.11)
  the two profiles are of different devices: /device:TPU:481 before, /device:TPU:353 now
where the time goes in v4:
time: 87.7 us; the launch traced here: 87.5 us
  Pallas kernels  84.6 us (96%)
  local copies, waits for them, and re-layouts  1.54 us (2%)
  between operations  1.34 us (2%)
    pallas_call x1, Pallas kernels, row_sums(): pl.pallas_call(row_kernel, out_shape=jax.ShapeDtypeStruct((2, 6, 128, 512...  83 us

profile of v4, /device:TPU:353, one launch (start us, length us, event | category | flops | bytes accessed | tf_op | source)
XLA Modules:
  0.0 87.5 jit_solution(2396036228121799867)
XLA Ops:
  1.3 0.7 gather_panel.1
  2.0 0.0 copy-start
  2.0 0.0 copy-start.1
  2.0 0.0 copy-start.2
  2.1 0.0 copy-start.3
  2.1 1.0 %conditional.1 = (bf16[3,2,96,512]{3,2,1,0:T(8,128)(2,1)S(1)}) conditional(s32[]{:T(128)} %bitcast.1, bf16[6,2,96,512]{3,2,1,0:T(8,128)(2,1)S(1)} %gather_panel.1, bf16[6,2,96,512]{3,2,1,0:T(8,128)(2,1)S(1)} %gather_panel.1, bf16[6,2,96,512]{3,2,1,0:T(8,128)(2,1)S(1)} %gather_panel.1, ...), branch_computations={%region_0.0_spmd, %region_1.0_spmd, %region_2.0_spmd, %region_3.0_... | conditional | bytes 8 | solution.py:541
  2.1 0.9 %send_home.19 = bf16[3,2,96,512]{3,2,1,0:T(8,128)(2,1)S(1)} custom-call(bf16[6,2,96,512]{3,2,1,0:T(8,128)(2,1)S(1)} %panel_ref.3), custom_call_target="tpu_custom_call" | custom-call | tf_op jit(solution)/shard_map/cond/branch_3_fun/send_home/pallas_call | solution.py:181
  3.0 0.1 copy-done
  3.2 0.1 copy-done.1
  3.3 0.0 copy-done.2
  3.3 0.0 copy-done.3
  3.3 83.0 %row_sums.1 = bf16[2,6,128,512]{3,2,1,0:T(8,128)(2,1)S(1)} custom-call(s32[3,6]{1,0:T(4,128)S(1)} %bitcast.7, s32[1]{0:T(128)S(6)} %copy.25.step_ref, bf16[6,3,96,512]{3,2,1,0:T(8,128)(2,1)} %left_hbm.1, bf16[6,3,96,512]{3,2,1,0:T(8,128)(2,1)} %right_hbm.1, bf16[6,128,512]{2,1,0:T(8,128)(2,1)S(1)} %copy-done, ...), custom_call_target="tpu_custom_call" | custom-call | tf_op jit(solution)/shard_map/row_sums/pallas_call | solution.py:499
  86.3 1.2 %slice_bitcast_fusion = (bf16[6,128,512]{2,1,0:T(8,128)(2,1)}, bf16[6,128,512]{2,1,0:T(8,128)(2,1)}) fusion(bf16[2,6,128,512]{3,2,1,0:T(8,128)(2,1)S(1)} %row_sums.1), kind=kLoop, calls=%fused_computation | loop fusion | bytes 3145728 | tf_op jit(solution)/shard_map/squeeze | solution.py:545
Async XLA Ops:
  2.0 1.1 %copy-start = (bf16[6,128,512]{2,1,0:T(8,128)(2,1)S(1)}, bf16[6,128,512]{2,1,0:T(8,128)(2,1)}, u32[]{:S(2)}) copy-start(bf16[6,128,512]{2,1,0:T(8,128)(2,1)} %probe_hbm.1) | copy-start | bytes 2359300
  2.0 1.3 %copy-start.1 = (bf16[512,512]{1,0:T(8,128)(2,1)S(1)}, bf16[512,512]{1,0:T(8,128)(2,1)}, u32[]{:S(2)}) copy-start(bf16[512,512]{1,0:T(8,128)(2,1)} %solve_ref.1) | copy-start | bytes 1572868
  2.0 1.3 %copy-start.2 = (bf16[512,128]{1,0:T(8,128)(2,1)S(1)}, bf16[512,128]{1,0:T(8,128)(2,1)}, u32[]{:S(2)}) copy-start(bf16[512,128]{1,0:T(8,128)(2,1)} %sketch_ref.1) | copy-start | bytes 393220
  2.1 1.3 %copy-start.3 = (s32[6,3]{0,1:T(4,128)S(1)}, s32[6,3]{0,1:T(4,128)}, u32[]{:S(2)}) copy-start(s32[6,3]{0,1:T(4,128)} %param.25) | copy-start | bytes 220

commit v5 on v4

--- a/solution.py
+++ b/solution.py
@@ -130,71 +130,6 @@
     )(ranks, step, left, right)
 
 
-def home_kernel(owner, panel_ref, out_ref, send_sem, recv_sem, local_sem):
-    z = lax.axis_index("row")
-    c = lax.axis_index("col")
-    owner_line = owner // 2
-    owner_core = owner % 2
-    is_owner = c == owner
-    is_home = (c // 2 == z) & jnp.logical_not(is_owner)
-    holds_own = is_owner & (z == owner_line)
-    barrier = pltpu.get_barrier_semaphore()
-
-    @pl.when(is_home)
-    def _():
-        pl.semaphore_signal(barrier, inc=1, device_id=(z, owner), device_id_type=MESH)
-
-    def copy(core):
-        part = panel_ref.at[pl.ds(3 * core, 3)]
-        return remote(part, out_ref, send_sem.at[core], recv_sem, (z, 2 * z + core))
-
-    @pl.when(is_owner)
-    def _():
-        pl.semaphore_wait(barrier, jnp.where(z == owner_line, 1, 2))
-
-    for core in range(2):
-        flag = is_owner if core != owner_core else is_owner & (z != owner_line)
-
-        @pl.when(flag)
-        def _(core=core):
-            copy(core).start()
-
-    @pl.when(holds_own)
-    def _():
-        own = pltpu.make_async_copy(panel_ref.at[pl.ds(3 * owner_core, 3)], out_ref, local_sem)
-        own.start()
-        own.wait()
-
-    @pl.when(is_home)
-    def _():
-        remote(out_ref, out_ref, send_sem.at[0], recv_sem, (z, owner)).wait_recv()
-
-    for core in range(2):
-        flag = is_owner if core != owner_core else is_owner & (z != owner_line)
-
-        @pl.when(flag)
-        def _(core=core):
-            copy(core).wait_send()
-
-
-def send_home(owner, panel):
-    return pl.pallas_call(
-        functools.partial(home_kernel, owner),
-        out_shape=jax.ShapeDtypeStruct((3, 2, 96, 512), BF16),
-        in_specs=[pl.BlockSpec(memory_space=pltpu.VMEM)],
-        out_specs=pl.BlockSpec(memory_space=pltpu.VMEM),
-        scratch_shapes=[
-            pltpu.SemaphoreType.DMA((2,)),
-            pltpu.SemaphoreType.DMA,
-            pltpu.SemaphoreType.DMA,
-        ],
-        compiler_params=pltpu.CompilerParams(
-            collective_id=owner - 15, has_side_effects=True, vmem_limit_bytes=16 * 2**20
-        ),
-        name="send_home",
-    )(panel)
-
-
 def dot_nt(a, b):
     return lax.dot_general(a, b, (((1,), (1,)), ((), ())), preferred_element_type=F32)
 
@@ -208,10 +143,11 @@
 
 
 def row_kernel(
-    ranks_ref, step_ref, left_hbm, right_hbm, probe_hbm, home_ref, sketch_ref, solve_ref, out_ref,
-    upper_ref, left_ref, right_ref, probe_ref, probed_ref, stack_ref, reduced_ref,
+    owner, ranks_ref, step_ref, left_hbm, right_hbm, probe_hbm, panel_ref, sketch_ref, solve_ref, out_ref,
+    upper_ref, extra_ref, left_ref, right_ref, probe_ref, probed_ref, stack_ref, reduced_ref,
     range_ref, co_ref, send_ref, got_ref, acc_ref, cur_ref, a_ref, b_ref,
-    home_sem, up_send, down_send, chunk_sem, load_sem, send_sem, recv_sem, pair_send, pair_recv,
+    src_send, up_send, down_send, chunk_sem, extra_up_send, extra_down_send, extra_recv, give_send,
+    local_sem, load_sem, send_sem, recv_sem, pair_send, pair_recv,
 ):
     z = lax.axis_index("row")
     c = lax.axis_index("col")
@@ -278,37 +214,97 @@
             pltpu.make_async_copy(probe_hbm.at[rows], probe_ref.at[rows], load_sem.at[2, g]),
         ]
 
-    line = c // 2
-    home = z == line
+    s = c // 2
+    kind = c % 2
+    owner_line = owner // 2
+    owner_core = owner % 2
+    carrier = owner + 1 - 2 * owner_core
+    home = z == s
+    is_owner = c == owner
+    is_carrier = c == carrier
     target = z >= FIRST
-    parent, first, second = (look_up(words, line, z) for words in tree_tables())
-    receives = parent != z
-    up = first != z
-    down = second != z
+    parent, first, second = (look_up(words, s, z) for words in tree_tables())
+    plain = jnp.logical_not(is_owner)
+    up = plain & (first != z)
+    down = plain & (second != z)
+    from_owner = home & plain
+    from_parent = plain & (parent != z)
+    from_carrier = is_owner & target & (z != owner_line)
+    receives = from_owner | from_parent | from_carrier
+    sends_home = is_owner & (z != owner_line)
+    holds_own = is_owner & (z == owner_line)
+    extra_up = is_carrier & (first != z)
+    extra_down = is_carrier & (second != z)
+    extra_gives = is_carrier & target & (z != owner_line)
+    extra_takes = is_carrier & (home | (parent != z))
 
     def piece(q):
         return q // 4, (q // 2) % 2, pl.ds(pl.multiple_of((q % 2) * HALF, HALF), HALF)
 
-    def chunk_copy(ref, sems, plane, q):
+    def src_copy(core, q):
         t, side, rows = piece(q)
         return remote(
-            ref.at[t, side, rows], upper_ref.at[t, side, rows], sems.at[q], chunk_sem.at[q], (plane, c)
+            panel_ref.at[3 * core + t, side, rows],
+            upper_ref.at[t, side, rows],
+            src_send.at[core, q],
+            chunk_sem.at[q],
+            (z, 2 * z + core),
         )
 
-    def forward(ref, q):
-        @pl.when(up)
+    def lend_copy(q):
+        t, side, rows = piece(q)
+        return remote(
+            panel_ref.at[3 * owner_core + t, side, rows],
+            extra_ref.at[t, side, rows],
+            src_send.at[owner_core, q],
+            extra_recv.at[q],
+            (z, carrier),
+        )
+
+    def chain_copy(ref, send, recv, device, q):
+        t, side, rows = piece(q)
+        here = ref.at[t, side, rows]
+        return remote(here, here, send.at[q], recv.at[q], device)
+
+    def hand_copy(q):
+        t, side, rows = piece(q)
+        return remote(
+            extra_ref.at[t, side, rows], upper_ref.at[t, side, rows], give_send.at[q], chunk_sem.at[q], (z, owner)
+        )
+
+    def up_copy(q):
+        return chain_copy(upper_ref, up_send, chunk_sem, (first, c), q)
+
+    def down_copy(q):
+        return chain_copy(upper_ref, down_send, chunk_sem, (second, c), q)
+
+    def extra_up_copy(q):
+        return chain_copy(extra_ref, extra_up_send, extra_recv, (first, c), q)
+
+    def extra_down_copy(q):
+        return chain_copy(extra_ref, extra_down_send, extra_recv, (second, c), q)
+
+    def loop(flag, body):
+        @pl.when(flag)
         def _():
-            chunk_copy(ref, up_send, first, q).start()
-
-        @pl.when(down)
+            lax.fori_loop(0, CHUNKS, lambda q, _: (body(q), 0)[1], 0)
+
+    def when(flag, body):
+        @pl.when(flag)
         def _():
-            chunk_copy(ref, down_send, second, q).start()
+            body()
 
     def relay(q):
-        @pl.when(receives)
+        when(receives, lambda: chain_copy(upper_ref, up_send, chunk_sem, (z, c + 1 - 2 * kind), q).wait_recv())
+        when(up, lambda: up_copy(q).start())
+        when(down, lambda: down_copy(q).start())
+
+        @pl.when(extra_takes)
         def _():
-            chunk_copy(upper_ref, up_send, parent, q).wait_recv()
-            forward(upper_ref, q)
+            chain_copy(extra_ref, extra_up_send, extra_recv, (z, owner), q).wait_recv()
+            when(extra_up, lambda: extra_up_copy(q).start())
+            when(extra_down, lambda: extra_down_copy(q).start())
+            when(extra_gives, lambda: hand_copy(q).start())
 
     def keep_of(a, t):
         tile = c * 3 + t
@@ -348,9 +344,11 @@
             range_ref[a] += dot_nn(mixed, left_ref[a, t])
             co_ref[a] += dot_nn(folded, closing)
 
-            @pl.when((t < 2) & (g < 2))
-            def _(k=k):
-                relay(t * 4 + 4 + g * 2 + k)
+            q = 4 + t * 6 + g * GROUP + k
+
+            @pl.when(q < CHUNKS)
+            def _(q=q):
+                relay(q)
 
     def close_rows(g):
         for k in range(GROUP):
@@ -409,32 +407,51 @@
 
     barrier = pltpu.get_barrier_semaphore()
 
-    @pl.when(receives)
-    def _():
-        pl.semaphore_signal(barrier, inc=1, device_id=(parent, c), device_id_type=MESH)
+    def greet(flag, device):
+        @pl.when(flag)
+        def _():
+            pl.semaphore_signal(barrier, inc=1, device_id=device, device_id_type=MESH)
+
+    greet(from_owner, (z, owner))
+    greet(from_parent, (parent, c))
+    greet(from_carrier, (z, carrier))
 
     @pl.when(target)
     def _():
         for device in (sibling, *firsts, *seconds):
             pl.semaphore_signal(barrier, inc=1, device_id=device, device_id_type=MESH)
 
-    peers = jnp.where(up, 1, 0) + jnp.where(down, 1, 0) + jnp.where(target, 7, 0)
+    def count(flag, amount=1):
+        return jnp.where(flag, amount, 0)
+
+    peers = (
+        count(is_owner, jnp.where(z == owner_line, 1, 2))
+        + count(up)
+        + count(down)
+        + count(extra_gives)
+        + count(target, 7)
+    )
 
     @pl.when(peers > 0)
     def _():
         pl.semaphore_wait(barrier, peers)
 
-    @pl.when(home)
-    def _():
-        own = pltpu.make_async_copy(home_ref, upper_ref, home_sem)
-        own.start()
-        lax.fori_loop(0, CHUNKS, lambda q, _: (forward(home_ref, q), 0)[1], 0)
-        own.wait()
+    loop(holds_own, lambda q: lend_copy(q).start())
+    for half in range(2):
+        flag = is_owner if half != owner_core else sends_home
+        loop(flag, lambda q, half=half: src_copy(half, q).start())
+
+    @pl.when(holds_own)
+    def _():
+        copy = pltpu.make_async_copy(panel_ref.at[pl.ds(3 * owner_core, 3)], upper_ref, local_sem)
+        copy.start()
+        copy.wait()
 
     @pl.when(jnp.logical_not(target))
     def _():
         out_ref[...] = jnp.zeros_like(out_ref)
-        lax.fori_loop(0, CHUNKS, lambda q, _: (relay(q), 0)[1], 0)
+
+    loop(jnp.logical_not(target), relay)
 
     @pl.when(target)
     def _():
@@ -479,29 +496,28 @@
 
         lax.fori_loop(0, GROUPS, finish, 0)
 
-    @pl.when(up)
-    def _():
-        lax.fori_loop(
-            0, CHUNKS, lambda q, _: (chunk_copy(upper_ref, up_send, first, q).wait_send(), 0)[1], 0
-        )
-
-    @pl.when(down)
-    def _():
-        lax.fori_loop(
-            0, CHUNKS, lambda q, _: (chunk_copy(upper_ref, down_send, second, q).wait_send(), 0)[1], 0
-        )
-
-
-def row_sums(ranks, step, left, right, probes, home, sketch, solve):
+    loop(holds_own, lambda q: lend_copy(q).wait_send())
+    for half in range(2):
+        flag = is_owner if half != owner_core else sends_home
+        loop(flag, lambda q, half=half: src_copy(half, q).wait_send())
+    loop(up, lambda q: up_copy(q).wait_send())
+    loop(down, lambda q: down_copy(q).wait_send())
+    loop(extra_up, lambda q: extra_up_copy(q).wait_send())
+    loop(extra_down, lambda q: extra_down_copy(q).wait_send())
+    loop(extra_gives, lambda q: hand_copy(q).wait_send())
+
+
+def row_sums(owner, ranks, step, left, right, probes, panel, sketch, solve):
     vmem = pl.BlockSpec(memory_space=pltpu.VMEM)
     smem = pl.BlockSpec(memory_space=pltpu.SMEM)
     hbm = pl.BlockSpec(memory_space=pl.ANY)
     return pl.pallas_call(
-        row_kernel,
+        functools.partial(row_kernel, owner),
         out_shape=jax.ShapeDtypeStruct((2, 6, 128, 512), BF16),
         in_specs=[smem, smem, hbm, hbm, hbm, vmem, vmem, vmem],
         out_specs=vmem,
         scratch_shapes=[
+            pltpu.VMEM((3, 2, 96, 512), BF16),
             pltpu.VMEM((3, 2, 96, 512), BF16),
             pltpu.VMEM((6, 3, 96, 512), BF16),
             pltpu.VMEM((6, 3, 96, 512), BF16),
@@ -517,10 +533,9 @@
             pltpu.VMEM((6, 128, 512), BF16),
             pltpu.VMEM((GROUPS, 3, GROUP, 32, 512), BF16),
             pltpu.VMEM((GROUPS, 4, GROUP, 32, 512), BF16),
+            pltpu.SemaphoreType.DMA((2, CHUNKS)),
+            *[pltpu.SemaphoreType.DMA((CHUNKS,))] * 7,
             pltpu.SemaphoreType.DMA,
-            pltpu.SemaphoreType.DMA((CHUNKS,)),
-            pltpu.SemaphoreType.DMA((CHUNKS,)),
-            pltpu.SemaphoreType.DMA((CHUNKS,)),
             pltpu.SemaphoreType.DMA((3, GROUPS)),
             pltpu.SemaphoreType.DMA((GROUPS, 3, 3)),
             pltpu.SemaphoreType.DMA((GROUPS, 3, 3)),
@@ -528,19 +543,19 @@
             pltpu.SemaphoreType.DMA((2, GROUPS)),
         ],
         compiler_params=pltpu.CompilerParams(
-            collective_id=0, has_side_effects=True, vmem_limit_bytes=50 * 2**20
+            collective_id=owner - 16, has_side_effects=True, vmem_limit_bytes=50 * 2**20
         ),
         name="row_sums",
-    )(ranks, step, left, right, probes, home, sketch, solve)
+    )(ranks, step, left, right, probes, panel, sketch, solve)
 
 
 def body(left_factors, right_factors, ranks, sketch_left, sketch_right, upper_inverse, step):
     slots = ranks.T
     panel = gather_panel(slots, step, left_factors, right_factors)
-    branches = [functools.partial(send_home, owner) for owner in range(16, 32)]
-    home = lax.switch(lax.div(step[0], 3) - 16, branches, panel)
-    out = row_sums(
-        slots, step, left_factors, right_factors, sketch_left, home, sketch_right, upper_inverse
+    branches = [functools.partial(row_sums, owner) for owner in range(16, 32)]
+    out = lax.switch(
+        lax.div(step[0], 3) - 16, branches, slots, step, left_factors, right_factors, sketch_left,
+        panel, sketch_right, upper_inverse,
     )
     return (out[0], out[1])
 

time: 87.7 us -> 95.5 us (1.089)
  the two profiles are of different devices: /device:TPU:353 before, /device:TPU:449 now
where the time goes in v5:
time: 95.5 us; the launch traced here: 95.3 us
  Pallas kernels  81.1 us (85%)
  loops' own time  10.3 us (11%)
  local copies, waits for them, and re-layouts  2.62 us (3%)
  between operations  1.35 us (1%)
    pallas_call x1, Pallas kernels, row_sums(): pl.pallas_call(functools.partial(row_kernel, owner), out_shape=jax.ShapeD...  79.2 us
    another operation x1, loops' own time, body(): lax.switch(lax.div(step[0], 3) - 16, branches, slots, step, left_factors,...  10.3 us
    squeeze x1, local copies, waits for them, and re-layouts, body(): return (out[0], out[1])  2.61 us

profile of v5, /device:TPU:449, one launch (start us, length us, event | category | flops | bytes accessed | tf_op | source)
XLA Modules:
  0.0 95.3 jit_solution(11739160247415830510)
XLA Ops:
  1.3 0.0 copy-start
  1.3 0.0 copy-start.1
  1.3 0.0 copy-start.2
  1.3 1.9 %gather_panel.1 = bf16[6,2,96,512]{3,2,1,0:T(8,128)(2,1)} custom-call(s32[3,6]{1,0:T(4,128)} %bitcast.6, s32[1]{0:T(128)S(6)} %copy.73.step_ref, bf16[6,3,96,512]{3,2,1,0:T(8,128)(2,1)} %left_ref.1, bf16[6,3,96,512]{3,2,1,0:T(8,128)(2,1)} %right_ref.1), custom_call_target="tpu_custom_call" | custom-call | tf_op jit(solution)/shard_map/gather_panel/pallas_call | solution.py:117
  3.2 0.0 copy-done
  3.2 0.0 copy-done.1
  3.2 0.0 copy-done.2
  3.2 89.5 %conditional.1 = (bf16[2,6,128,512]{3,2,1,0:T(8,128)(2,1)}) conditional(s32[]{:T(128)} %bitcast, (s32[3,6]{1,0:T(4,128)S(1)}, s32[1]{0:T(128)}, bf16[6,3,96,512]{3,2,1,0:T(8,128)(2,1)S(1)}, bf16[6,3,96,512]{3,2,1,0:T(8,128)(2,1)}, bf16[6,128,512]{2,1,0:T(8,128)(2,1)}, /*index=5*/bf16[6,2,96,512]{3,2,1,0:T(8,128)(2,1)}, ...), branch_computations={%region_0.0_spmd, %region_1.0_spmd, %region_2.0_spmd, %region_3.0_... | conditional | bytes 8 | solution.py:556
  12.4 79.2 %row_sums.24 = bf16[2,6,128,512]{3,2,1,0:T(8,128)(2,1)} custom-call(s32[3,6]{1,0:T(4,128)S(1)} %get-tuple-element.337.ranks_ref, s32[1]{0:T(128)} %get-tuple-element.338.step_ref, bf16[6,3,96,512]{3,2,1,0:T(8,128)(2,1)S(1)} %get-tuple-element.339.left_hbm, bf16[6,3,96,512]{3,2,1,0:T(8,128)(2,1)} %get-tuple-element.340.right_hbm, ...), custom_call_target="tpu_custom_call" | custom-call | tf_op jit(solution)/shard_map/cond/branch_8_fun/row_sums/pallas_call | solution.py:514
  92.7 2.6 %slice_bitcast_fusion = (bf16[6,128,512]{2,1,0:T(8,128)(2,1)}, bf16[6,128,512]{2,1,0:T(8,128)(2,1)}) fusion(bf16[2,6,128,512]{3,2,1,0:T(8,128)(2,1)} %get-tuple-element.501), kind=kLoop, calls=%fused_computation | loop fusion | bytes 3145728 | tf_op jit(solution)/shard_map/squeeze | solution.py:560
Async XLA Ops:
  1.3 1.9 %copy-start = (bf16[6,3,96,512]{3,2,1,0:T(8,128)(2,1)S(1)}, bf16[6,3,96,512]{3,2,1,0:T(8,128)(2,1)}, u32[]{:S(2)}) copy-start(bf16[6,3,96,512]{3,2,1,0:T(8,128)(2,1)} %left_ref.1) | copy-start | bytes 5308420
  1.3 1.9 %copy-start.1 = (bf16[512,128]{1,0:T(8,128)(2,1)S(1)}, bf16[512,128]{1,0:T(8,128)(2,1)}, u32[]{:S(2)}) copy-start(bf16[512,128]{1,0:T(8,128)(2,1)} %param.27) | copy-start | bytes 393220
  1.3 1.9 %copy-start.2 = (s32[6,3]{0,1:T(4,128)S(1)}, s32[6,3]{0,1:T(4,128)}, u32[]{:S(2)}) copy-start(s32[6,3]{0,1:T(4,128)} %param.25) | copy-start | bytes 220

commit v6 on v3

--- a/solution.py
+++ b/solution.py
@@ -12,8 +12,8 @@
 BF16 = jnp.bfloat16
 FIRST = 8
 LAST = 15
-HALF = 48
-CHUNKS = 12
+PIECE = 32
+CHUNKS = 18
 
 
 def remote(src, dst, send_sem, recv_sem, device):
@@ -28,34 +28,31 @@
 
 
 def line_trees():
+    paths = {
+        0: [(0, 4, 9, 8), (9, 10), (0, 14, 15), (14, 13, 12, 11)],
+        1: [(1, 8, 9, 10), (1, 14, 15), (14, 13, 12, 11)],
+        2: [(2, 8, 9, 10), (2, 14, 15), (14, 13, 12, 11)],
+        3: [(3, 9, 8), (9, 10, 11), (3, 14, 15), (14, 13, 12)],
+        4: [(4, 9, 8), (9, 10, 11), (4, 14, 15), (14, 13, 12)],
+        5: [(5, 9, 8), (9, 10, 11, 12), (5, 15, 14, 13)],
+        6: [(6, 9, 8), (9, 10, 11, 12), (6, 15, 14, 13)],
+        7: [(7, 9, 8), (9, 10, 11, 12), (7, 3, 14, 15), (14, 13)],
+        8: [(8, 9, 10, 11, 12, 13), (8, 2, 15, 14)],
+        9: [(9, 10, 11, 12, 13, 14), (9, 8, 2, 15)],
+        10: [(10, 11, 12, 13, 14, 15), (10, 9, 8)],
+        11: [(11, 12, 13, 14, 15), (11, 10, 9, 8)],
+        12: [(12, 13, 14, 15), (12, 11, 10, 9, 8)],
+        13: [(13, 14, 15), (13, 12, 11, 10, 9, 8)],
+        14: [(14, 13, 12, 11, 10, 9), (14, 15, 5, 8)],
+        15: [(15, 14, 13, 12, 11, 10), (15, 5, 8, 9)],
+    }
     trees = []
     for s in range(16):
         parent = {}
-
-        def chain(*planes):
-            for before, after in zip(planes, planes[1:]):
+        for path in paths[s]:
+            for before, after in zip(path, path[1:]):
+                assert after not in parent and after != s
                 parent[after] = before
-
-        low = s < FIRST
-        if low or s == 15:
-            chain(*((s, 4, 9) if s < 2 else (s, 5, 9) if s == 15 else (s, 9)), 10, 11)
-            chain(9, 8)
-        if low or s == 8:
-            chain(*((s, 3, 14) if 6 <= s < 8 else (s, 2, 14) if s == 8 else (s, 14)), 13, 12)
-            chain(14, 15)
-        if s == 8:
-            chain(8, 9, 10, 11)
-        if s == 15:
-            chain(15, 14, 13, 12)
-        if s == 9:
-            chain(9, 10, 11, 12, 13)
-            chain(9, 8, 2, 15, 14)
-        if s == 14:
-            chain(14, 13, 12, 11, 10)
-            chain(14, 15, 5, 8, 9)
-        if 10 <= s <= 13:
-            chain(*range(s, 16))
-            chain(*range(s, 7, -1))
         trees.append(parent)
     return trees
 
@@ -186,7 +183,7 @@
         pl.semaphore_wait(barrier, peers)
 
     def piece(q):
-        return q // 4, (q // 2) % 2, pl.ds(pl.multiple_of((q % 2) * HALF, HALF), HALF)
+        return q // 6, (q // 3) % 2, pl.ds(pl.multiple_of((q % 3) * PIECE, PIECE), PIECE)
 
     def src_copy(core, q):
         t, side, rows = piece(q)
@@ -316,7 +313,7 @@
 
 def row_kernel(
     ranks_ref, step_ref, left_hbm, right_hbm, probe_hbm, upper_ref, sketch_ref, solve_ref, out_ref,
-    left_ref, right_ref, probe_ref, stack_ref, reduced_ref,
+    left_ref, right_ref, probe_ref, reduced_ref,
     send_ref, got_ref, acc_ref, cur_ref, a_ref, b_ref,
     load_sem, send_sem, recv_sem, pair_send, pair_recv,
 ):
@@ -392,18 +389,18 @@
         level = lax.broadcasted_iota(jnp.int32, (128, 96), 1)
         tiles = [c * 3 + j for j in range(3)]
         both = [
-            dot_nt(right_ref[members(g), j].reshape(GROUP * 96, 512), stack_ref[j]) for j in range(3)
+            dot_nt(right_ref[members(g), j].reshape(GROUP * 96, 512), upper_ref[j, 0]) for j in range(3)
         ]
         for k in range(GROUP):
             a = g * GROUP + k
             part = slice(96 * k, 96 * (k + 1))
             live = z * 6 + a > column
-            own_reduced = jnp.where(
+            own_right = jnp.where(
                 tiles[0] == column,
-                both[0][part, :128],
-                jnp.where(tiles[1] == column, both[1][part, :128], both[2][part, :128]),
+                right_ref[a, 0],
+                jnp.where(tiles[1] == column, right_ref[a, 1], right_ref[a, 2]),
             )
-            own_mixed = -own_reduced.T
+            own_mixed = -dot_nn(own_right, sketch_ref[...]).T
             range_sum = jnp.zeros((128, 512), F32)
             co_sum = jnp.zeros((128, 512), F32)
             for j in range(3):
@@ -411,14 +408,14 @@
                 depth = jnp.where(live & (tiles[j] <= column), ranks_ref[j, a], 0)
                 keep = level < depth
                 left = left_ref[a, j]
-                coupled = both[j][part, 128:].astype(BF16)
+                coupled = both[j][part].astype(BF16)
                 mixed = jnp.where(own, own_mixed, dot_nt(reduced_ref[j], coupled))
                 mixed = jnp.where(keep, mixed, 0.0).astype(BF16)
                 probed = dot_nt(probe_ref[a], left)
                 probed = jnp.where(keep, probed, 0.0).astype(BF16)
                 folded = dot_nn(probed, coupled).astype(BF16)
                 folded = jnp.where(own, -probed, folded)
-                closing = jnp.where(own, right_ref[a, j], upper_ref[j, 1])
+                closing = jnp.where(own, own_right, upper_ref[j, 1])
                 range_sum += dot_nn(mixed, left)
                 co_sum += dot_nn(folded, closing)
             acc_ref[a] = -jnp.where(even, range_sum, co_sum)
@@ -479,10 +476,7 @@
         barrier = pltpu.get_barrier_semaphore()
         for device in (sibling, *firsts, *seconds):
             pl.semaphore_signal(barrier, inc=1, device_id=device, device_id_type=MESH)
-        flat = sketch_ref[...].astype(F32).T.astype(BF16)
         for j in range(3):
-            stack_ref[j, :128] = flat
-            stack_ref[j, 128:] = upper_ref[j, 0]
             reduced = dot_nn(upper_ref[j, 1], sketch_ref[...]).astype(BF16).astype(F32)
             reduced_ref[j] = reduced.T.astype(BF16)
         pl.semaphore_wait(barrier, 7)
@@ -527,7 +521,6 @@
             pltpu.VMEM((6, 3, 96, 512), BF16),
             pltpu.VMEM((6, 3, 96, 512), BF16),
             pltpu.VMEM((6, 128, 512), BF16),
-            pltpu.VMEM((3, 224, 512), BF16),
             pltpu.VMEM((3, 128, 96), BF16),
             pltpu.VMEM((6, 128, 512), BF16),
             pltpu.VMEM((6, 128, 512), BF16),

time: 78.7 us -> 76.5 us (0.972); the launches traced: 77.5 us -> 77 us
    pallas_call x1, Pallas kernels: 26.6 us -> 23.9 us  [spread_panel(): pl.pallas_call(functools.partial(panel_kernel, owner), out_shape=jax.Shap...]
    pallas_call x1, Pallas kernels: 47.5 us -> 49.6 us  [row_sums(): pl.pallas_call(row_kernel, out_shape=jax.ShapeDtypeStruct((2, 6, 128, 512...]
where the time goes in v6:
time: 76.5 us; the launch traced here: 77 us
  Pallas kernels  74.3 us (97%)
  between operations  1.37 us (2%)
  local copies, waits for them, and re-layouts  1.27 us (2%)
    pallas_call x1, Pallas kernels, row_sums(): pl.pallas_call(row_kernel, out_shape=jax.ShapeDtypeStruct((2, 6, 128, 512...  49.6 us
    pallas_call x1, Pallas kernels, spread_panel(): pl.pallas_call(functools.partial(panel_kernel, owner), out_shape=jax.Shap...  23.9 us

profile of v6, /device:TPU:481, one launch (start us, length us, event | category | flops | bytes accessed | tf_op | source)
XLA Modules:
  0.0 77.0 jit_solution(7245636783508401836)
XLA Ops:
  1.3 0.7 gather_panel.1
  2.0 0.0 copy-start
  2.0 0.0 copy-start.1
  2.0 0.0 copy-start.2
  2.1 0.0 copy-start.3
  2.1 24.0 %conditional.1 = (bf16[3,2,96,512]{3,2,1,0:T(8,128)(2,1)S(1)}) conditional(s32[]{:T(128)} %bitcast.1, bf16[6,2,96,512]{3,2,1,0:T(8,128)(2,1)S(1)} %gather_panel.1, bf16[6,2,96,512]{3,2,1,0:T(8,128)(2,1)S(1)} %gather_panel.1, bf16[6,2,96,512]{3,2,1,0:T(8,128)(2,1)S(1)} %gather_panel.1, ...), branch_computations={%region_0.0_spmd, %region_1.0_spmd, %region_2.0_spmd, %region_3.0_... | conditional | bytes 8 | solution.py:548
  2.1 23.9 %spread_panel.17 = bf16[3,2,96,512]{3,2,1,0:T(8,128)(2,1)S(1)} custom-call(bf16[6,2,96,512]{3,2,1,0:T(8,128)(2,1)S(1)} %panel_ref.1), custom_call_target="tpu_custom_call" | custom-call | tf_op jit(solution)/shard_map/cond/branch_1_fun/spread_panel/pallas_call | solution.py:278
  26.1 0.0 copy-done
  26.1 0.0 copy-done.1
  26.1 0.0 copy-done.2
  26.1 0.0 copy-done.3
  26.1 49.6 %row_sums.1 = bf16[2,6,128,512]{3,2,1,0:T(8,128)(2,1)S(1)} custom-call(s32[3,6]{1,0:T(4,128)S(1)} %bitcast.7, s32[1]{0:T(128)S(6)} %copy.25.step_ref, bf16[6,3,96,512]{3,2,1,0:T(8,128)(2,1)} %left_hbm.1, bf16[6,3,96,512]{3,2,1,0:T(8,128)(2,1)} %right_hbm.1, bf16[6,128,512]{2,1,0:T(8,128)(2,1)S(1)} %copy-done, ...), custom_call_target="tpu_custom_call" | custom-call | tf_op jit(solution)/shard_map/row_sums/pallas_call | solution.py:515
  75.8 1.2 %slice_bitcast_fusion = (bf16[6,128,512]{2,1,0:T(8,128)(2,1)}, bf16[6,128,512]{2,1,0:T(8,128)(2,1)}) fusion(bf16[2,6,128,512]{3,2,1,0:T(8,128)(2,1)S(1)} %row_sums.1), kind=kLoop, calls=%fused_computation | loop fusion | bytes 3145728 | tf_op jit(solution)/shard_map/squeeze | solution.py:552
Async XLA Ops:
  2.0 24.1 %copy-start = (bf16[6,128,512]{2,1,0:T(8,128)(2,1)S(1)}, bf16[6,128,512]{2,1,0:T(8,128)(2,1)}, u32[]{:S(2)}) copy-start(bf16[6,128,512]{2,1,0:T(8,128)(2,1)} %probe_hbm.1) | copy-start | bytes 2359300
  2.0 24.1 %copy-start.1 = (bf16[512,512]{1,0:T(8,128)(2,1)S(1)}, bf16[512,512]{1,0:T(8,128)(2,1)}, u32[]{:S(2)}) copy-start(bf16[512,512]{1,0:T(8,128)(2,1)} %solve_ref.1) | copy-start | bytes 1572868
  2.0 24.1 %copy-start.2 = (bf16[512,128]{1,0:T(8,128)(2,1)S(1)}, bf16[512,128]{1,0:T(8,128)(2,1)}, u32[]{:S(2)}) copy-start(bf16[512,128]{1,0:T(8,128)(2,1)} %sketch_ref.1) | copy-start | bytes 393220
  2.1 24.0 %copy-start.3 = (s32[6,3]{0,1:T(4,128)S(1)}, s32[6,3]{0,1:T(4,128)}, u32[]{:S(2)}) copy-start(s32[6,3]{0,1:T(4,128)} %param.25) | copy-start | bytes 220

commit v7 on v6

--- a/solution.py
+++ b/solution.py
@@ -12,8 +12,8 @@
 BF16 = jnp.bfloat16
 FIRST = 8
 LAST = 15
-PIECE = 32
-CHUNKS = 18
+PIECE = 48
+CHUNKS = 12
 
 
 def remote(src, dst, send_sem, recv_sem, device):
@@ -183,7 +183,7 @@
         pl.semaphore_wait(barrier, peers)
 
     def piece(q):
-        return q // 6, (q // 3) % 2, pl.ds(pl.multiple_of((q % 3) * PIECE, PIECE), PIECE)
+        return q // 4, (q // 2) % 2, pl.ds(pl.multiple_of((q % 2) * PIECE, PIECE), PIECE)
 
     def src_copy(core, q):
         t, side, rows = piece(q)
@@ -233,11 +233,6 @@
         def _():
             lax.fori_loop(0, CHUNKS, lambda q, _: (body(q), 0)[1], 0)
 
-    def when(flag, body):
-        @pl.when(flag)
-        def _():
-            body()
-
     loop(holds_own, lambda q: lend_copy(q).start())
     for core in range(2):
         flag = is_owner if core != owner_core else sends_home
@@ -249,19 +244,31 @@
         copy.start()
         copy.wait()
 
-    def relay(q):
-        when(receives, lambda: chain_copy(out_ref, up_send, recv_sem, (z, c + 1 - 2 * kind), q).wait_recv())
-        when(up, lambda: up_copy(q).start())
-        when(down, lambda: down_copy(q).start())
-
-        @pl.when(extra_takes)
-        def _():
-            chain_copy(extra_ref, extra_up_send, extra_recv, (z, owner), q).wait_recv()
-            when(extra_up, lambda: extra_up_copy(q).start())
-            when(extra_down, lambda: extra_down_copy(q).start())
-            when(extra_gives, lambda: give_copy(q).start())
-
-    lax.fori_loop(0, CHUNKS, lambda q, _: (relay(q), 0)[1], 0)
+    def relay(children, takes_extra=False, gives=False):
+        def body(q):
+            chain_copy(out_ref, up_send, recv_sem, (z, c + 1 - 2 * kind), q).wait_recv()
+            if children > 0:
+                up_copy(q).start()
+            if children > 1:
+                down_copy(q).start()
+            if takes_extra:
+                chain_copy(extra_ref, extra_up_send, extra_recv, (z, owner), q).wait_recv()
+                if children > 0:
+                    extra_up_copy(q).start()
+                if children > 1:
+                    extra_down_copy(q).start()
+                if gives:
+                    give_copy(q).start()
+
+        return body
+
+    roles = (jnp.logical_not(up), up & jnp.logical_not(down), down)
+    common = receives & jnp.logical_not(extra_takes)
+    for children, role in enumerate(roles):
+        loop(common & role, relay(children))
+        loop(extra_takes & extra_gives & role, relay(children, True, True))
+        if children:
+            loop(extra_takes & jnp.logical_not(extra_gives) & role, relay(children, True))
 
     loop(holds_own, lambda q: lend_copy(q).wait_send())
     for core in range(2):
@@ -307,8 +314,9 @@
     return jnp.dot(a, b, preferred_element_type=F32)
 
 
-GROUP = 2
-GROUPS = 6 // GROUP
+STARTS = (0, 3, 5)
+SIZES = (3, 2, 1)
+GROUPS = 3
 
 
 def row_kernel(
@@ -340,18 +348,18 @@
         return pl.ds(pl.multiple_of(((b + 4) % 4) * 32, 32), 32)
 
     def members(g):
-        return pl.ds(g * GROUP, GROUP)
+        return pl.ds(STARTS[g], SIZES[g])
 
     def copies(g, n, landing):
         made = []
         for k in range(3):
             by = k + 1
             if n == 0:
-                src, dst = cur_ref.at[members(g), rows32(u + by)], a_ref.at[g, k]
+                src, dst = cur_ref.at[members(g), rows32(u + by)], a_ref.at[k, members(g)]
                 if landing:
                     src = dst
             elif n == 1:
-                src = dst = b_ref.at[g, (v - by + 4) % 4 if landing else v]
+                src = dst = b_ref.at[(v - by + 4) % 4 if landing else v, members(g)]
             else:
                 src = dst = out_ref.at[core, members(g), rows32(u - by if landing else u)]
             device = seconds[k] if n == 1 else firsts[k]
@@ -389,10 +397,10 @@
         level = lax.broadcasted_iota(jnp.int32, (128, 96), 1)
         tiles = [c * 3 + j for j in range(3)]
         both = [
-            dot_nt(right_ref[members(g), j].reshape(GROUP * 96, 512), upper_ref[j, 0]) for j in range(3)
+            dot_nt(right_ref[members(g), j].reshape(SIZES[g] * 96, 512), upper_ref[j, 0]) for j in range(3)
         ]
-        for k in range(GROUP):
-            a = g * GROUP + k
+        for k in range(SIZES[g]):
+            a = STARTS[g] + k
             part = slice(96 * k, 96 * (k + 1))
             live = z * 6 + a > column
             own_right = jnp.where(
@@ -438,14 +446,14 @@
             arrive(g, 0)
             total = acc_ref[rows, rows32(u)]
             for k in range(3):
-                total += a_ref[g, k].astype(F32)
-            b_ref[g, v] = total.astype(BF16)
+                total += a_ref[k, rows].astype(F32)
+            b_ref[v, rows] = total.astype(BF16)
             start(g, 1)
         elif n == 2:
             arrive(g, 1)
-            total = b_ref[g, 0].astype(F32)
+            total = b_ref[0, rows].astype(F32)
             for b in range(1, 4):
-                total += b_ref[g, b].astype(F32)
+                total += b_ref[b, rows].astype(F32)
             block = total.astype(BF16)
 
             @pl.when(even)
@@ -454,8 +462,8 @@
 
             @pl.when(jnp.logical_not(even))
             def _():
-                solved = dot_nn(block.reshape(GROUP * 32, 512), solve_ref[...]).astype(BF16)
-                out_ref[1, rows, rows32(u)] = solved.reshape(GROUP, 32, 512)
+                solved = dot_nn(block.reshape(SIZES[g] * 32, 512), solve_ref[...]).astype(BF16)
+                out_ref[1, rows, rows32(u)] = solved.reshape(SIZES[g], 32, 512)
 
             start(g, 2)
         elif n == 3:
@@ -481,31 +489,18 @@
             reduced_ref[j] = reduced.T.astype(BF16)
         pl.semaphore_wait(barrier, 7)
 
-        def slot(t, _):
-            @pl.when(t < GROUPS)
-            def _():
+        for t in range(GROUPS + 5):
+            if t < GROUPS:
                 compute(t)
-
             for n in reversed(range(5)):
-                g = t - 1 - n
-
-                @pl.when((g >= 0) & (g < GROUPS))
-                def _(n=n, g=g):
-                    stage(n, g)
-
-            return 0
-
-        lax.fori_loop(0, GROUPS + 5, slot, 0)
-
-        def finish(g, _):
+                if 0 <= t - 1 - n < GROUPS:
+                    stage(n, t - 1 - n)
+        for g in range(GROUPS):
             pair_copy(g).wait_send()
             give_copy(g, core).wait_send()
             for n in range(3):
                 for copy in copies(g, n, False):
                     copy.wait_send()
-            return 0
-
-        lax.fori_loop(0, GROUPS, finish, 0)
 
 
 def row_sums(ranks, step, left, right, probes, upper, sketch, solve):
@@ -526,8 +521,8 @@
             pltpu.VMEM((6, 128, 512), BF16),
             pltpu.VMEM((6, 128, 512), F32),
             pltpu.VMEM((6, 128, 512), BF16),
-            pltpu.VMEM((GROUPS, 3, GROUP, 32, 512), BF16),
-            pltpu.VMEM((GROUPS, 4, GROUP, 32, 512), BF16),
+            pltpu.VMEM((3, 6, 32, 512), BF16),
+            pltpu.VMEM((4, 6, 32, 512), BF16),
             pltpu.SemaphoreType.DMA((3, GROUPS)),
             pltpu.SemaphoreType.DMA((GROUPS, 3, 3)),
             pltpu.SemaphoreType.DMA((GROUPS, 3, 3)),

time: 76.5 us -> 79.6 us (1.041)
  Pallas kernels: 74.3 us -> 76.6 us
    pallas_call x1, Pallas kernels: 23.9 us -> 25.1 us  [spread_panel(): pl.pallas_call(functools.partial(panel_kernel, owner), out_shape=jax.Shap...]
    pallas_call x1, Pallas kernels: 49.6 us -> 50.7 us  [row_sums(): pl.pallas_call(row_kernel, out_shape=jax.ShapeDtypeStruct((2, 6, 128, 512...]
where the time goes in v7:
time: 79.6 us; the launch traced here: 79.4 us
  Pallas kernels  76.6 us (96%)
  between operations  1.37 us (2%)
  local copies, waits for them, and re-layouts  1.27 us (2%)
    pallas_call x1, Pallas kernels, row_sums(): pl.pallas_call(row_kernel, out_shape=jax.ShapeDtypeStruct((2, 6, 128, 512...  50.7 us
    pallas_call x1, Pallas kernels, spread_panel(): pl.pallas_call(functools.partial(panel_kernel, owner), out_shape=jax.Shap...  25.1 us

profile of v7, /device:TPU:481, one launch (start us, length us, event | category | flops | bytes accessed | tf_op | source)
XLA Modules:
  0.0 79.4 jit_solution(6562010068364732418)
XLA Ops:
  1.3 0.7 gather_panel.1
  2.0 0.0 copy-start
  2.0 0.0 copy-start.1
  2.0 0.0 copy-start.2
  2.1 0.0 copy-start.3
  2.1 25.3 %conditional.1 = (bf16[3,2,96,512]{3,2,1,0:T(8,128)(2,1)S(1)}) conditional(s32[]{:T(128)} %bitcast.1, bf16[6,2,96,512]{3,2,1,0:T(8,128)(2,1)S(1)} %gather_panel.1, bf16[6,2,96,512]{3,2,1,0:T(8,128)(2,1)S(1)} %gather_panel.1, bf16[6,2,96,512]{3,2,1,0:T(8,128)(2,1)S(1)} %gather_panel.1, ...), branch_computations={%region_0.0_spmd, %region_1.0_spmd, %region_2.0_spmd, %region_3.0_... | conditional | bytes 8 | solution.py:543
  2.1 25.1 %spread_panel.26 = bf16[3,2,96,512]{3,2,1,0:T(8,128)(2,1)S(1)} custom-call(bf16[6,2,96,512]{3,2,1,0:T(8,128)(2,1)S(1)} %panel_ref.10), custom_call_target="tpu_custom_call" | custom-call | tf_op jit(solution)/shard_map/cond/branch_10_fun/spread_panel/pallas_call | solution.py:285
  27.4 0.0 copy-done
  27.4 0.0 copy-done.1
  27.4 0.0 copy-done.2
  27.4 0.0 copy-done.3
  27.4 50.7 %row_sums.1 = bf16[2,6,128,512]{3,2,1,0:T(8,128)(2,1)S(1)} custom-call(s32[3,6]{1,0:T(4,128)S(1)} %bitcast.7, s32[1]{0:T(128)S(6)} %copy.25.step_ref, bf16[6,3,96,512]{3,2,1,0:T(8,128)(2,1)} %left_hbm.1, bf16[6,3,96,512]{3,2,1,0:T(8,128)(2,1)} %right_hbm.1, bf16[6,128,512]{2,1,0:T(8,128)(2,1)S(1)} %copy-done, ...), custom_call_target="tpu_custom_call" | custom-call | tf_op jit(solution)/shard_map/row_sums/pallas_call | solution.py:510
  78.2 1.2 %slice_bitcast_fusion = (bf16[6,128,512]{2,1,0:T(8,128)(2,1)}, bf16[6,128,512]{2,1,0:T(8,128)(2,1)}) fusion(bf16[2,6,128,512]{3,2,1,0:T(8,128)(2,1)S(1)} %row_sums.1), kind=kLoop, calls=%fused_computation | loop fusion | bytes 3145728 | tf_op jit(solution)/shard_map/squeeze | solution.py:547
Async XLA Ops:
  2.0 25.4 %copy-start = (bf16[6,128,512]{2,1,0:T(8,128)(2,1)S(1)}, bf16[6,128,512]{2,1,0:T(8,128)(2,1)}, u32[]{:S(2)}) copy-start(bf16[6,128,512]{2,1,0:T(8,128)(2,1)} %probe_hbm.1) | copy-start | bytes 2359300
  2.0 25.4 %copy-start.1 = (bf16[512,512]{1,0:T(8,128)(2,1)S(1)}, bf16[512,512]{1,0:T(8,128)(2,1)}, u32[]{:S(2)}) copy-start(bf16[512,512]{1,0:T(8,128)(2,1)} %solve_ref.1) | copy-start | bytes 1572868
  2.0 25.4 %copy-start.2 = (bf16[512,128]{1,0:T(8,128)(2,1)S(1)}, bf16[512,128]{1,0:T(8,128)(2,1)}, u32[]{:S(2)}) copy-start(bf16[512,128]{1,0:T(8,128)(2,1)} %sketch_ref.1) | copy-start | bytes 393220
  2.1 25.4 %copy-start.3 = (s32[6,3]{0,1:T(4,128)S(1)}, s32[6,3]{0,1:T(4,128)}, u32[]{:S(2)}) copy-start(s32[6,3]{0,1:T(4,128)} %param.25) | copy-start | bytes 220

commit v8 on v6

--- a/solution.py
+++ b/solution.py
@@ -12,8 +12,8 @@
 BF16 = jnp.bfloat16
 FIRST = 8
 LAST = 15
-PIECE = 32
-CHUNKS = 18
+PIECE = 48
+CHUNKS = 12
 
 
 def remote(src, dst, send_sem, recv_sem, device):
@@ -183,7 +183,7 @@
         pl.semaphore_wait(barrier, peers)
 
     def piece(q):
-        return q // 6, (q // 3) % 2, pl.ds(pl.multiple_of((q % 3) * PIECE, PIECE), PIECE)
+        return q // 4, (q // 2) % 2, pl.ds(pl.multiple_of((q % 2) * PIECE, PIECE), PIECE)
 
     def src_copy(core, q):
         t, side, rows = piece(q)
@@ -233,11 +233,6 @@
         def _():
             lax.fori_loop(0, CHUNKS, lambda q, _: (body(q), 0)[1], 0)
 
-    def when(flag, body):
-        @pl.when(flag)
-        def _():
-            body()
-
     loop(holds_own, lambda q: lend_copy(q).start())
     for core in range(2):
         flag = is_owner if core != owner_core else sends_home
@@ -249,19 +244,31 @@
         copy.start()
         copy.wait()
 
-    def relay(q):
-        when(receives, lambda: chain_copy(out_ref, up_send, recv_sem, (z, c + 1 - 2 * kind), q).wait_recv())
-        when(up, lambda: up_copy(q).start())
-        when(down, lambda: down_copy(q).start())
-
-        @pl.when(extra_takes)
-        def _():
-            chain_copy(extra_ref, extra_up_send, extra_recv, (z, owner), q).wait_recv()
-            when(extra_up, lambda: extra_up_copy(q).start())
-            when(extra_down, lambda: extra_down_copy(q).start())
-            when(extra_gives, lambda: give_copy(q).start())
-
-    lax.fori_loop(0, CHUNKS, lambda q, _: (relay(q), 0)[1], 0)
+    def relay(children, takes_extra=False, gives=False):
+        def body(q):
+            chain_copy(out_ref, up_send, recv_sem, (z, c + 1 - 2 * kind), q).wait_recv()
+            if children > 0:
+                up_copy(q).start()
+            if children > 1:
+                down_copy(q).start()
+            if takes_extra:
+                chain_copy(extra_ref, extra_up_send, extra_recv, (z, owner), q).wait_recv()
+                if children > 0:
+                    extra_up_copy(q).start()
+                if children > 1:
+                    extra_down_copy(q).start()
+                if gives:
+                    give_copy(q).start()
+
+        return body
+
+    roles = (jnp.logical_not(up), up & jnp.logical_not(down), down)
+    common = receives & jnp.logical_not(extra_takes)
+    for children, role in enumerate(roles):
+        loop(common & role, relay(children))
+        loop(extra_takes & extra_gives & role, relay(children, True, True))
+        if children:
+            loop(extra_takes & jnp.logical_not(extra_gives) & role, relay(children, True))
 
     loop(holds_own, lambda q: lend_copy(q).wait_send())
     for core in range(2):
@@ -381,6 +388,8 @@
             pltpu.make_async_copy(right_hbm.at[rows], right_ref.at[rows], load_sem.at[1, g]),
             pltpu.make_async_copy(probe_hbm.at[rows], probe_ref.at[rows], load_sem.at[2, g]),
         ]
+
+    barrier = pltpu.get_barrier_semaphore()
 
     def compute(g):
         column = step_ref[0]
@@ -420,6 +429,11 @@
                 co_sum += dot_nn(folded, closing)
             acc_ref[a] = -jnp.where(even, range_sum, co_sum)
             send_ref[a] = -jnp.where(even, co_sum, range_sum).astype(BF16)
+
+        @pl.when(g == 0)
+        def _():
+            pl.semaphore_wait(barrier, 7)
+
         pair_copy(g).start()
 
     def stage(n, g):
@@ -473,13 +487,11 @@
         for g in range(GROUPS):
             for copy in loads(g):
                 copy.start()
-        barrier = pltpu.get_barrier_semaphore()
         for device in (sibling, *firsts, *seconds):
             pl.semaphore_signal(barrier, inc=1, device_id=device, device_id_type=MESH)
         for j in range(3):
             reduced = dot_nn(upper_ref[j, 1], sketch_ref[...]).astype(BF16).astype(F32)
             reduced_ref[j] = reduced.T.astype(BF16)
-        pl.semaphore_wait(barrier, 7)
 
         def slot(t, _):
             @pl.when(t < GROUPS)

time: 76.5 us -> 76.8 us (level)
  the two profiles are of different devices: /device:TPU:481 before, /device:TPU:417 now
where the time goes in v8:
time: 76.8 us; the launch traced here: 76.7 us
  Pallas kernels  74 us (96%)
  between operations  1.37 us (2%)
  local copies, waits for them, and re-layouts  1.27 us (2%)
    pallas_call x1, Pallas kernels, row_sums(): pl.pallas_call(row_kernel, out_shape=jax.ShapeDtypeStruct((2, 6, 128, 512...  44.5 us
    pallas_call x1, Pallas kernels, spread_panel(): pl.pallas_call(functools.partial(panel_kernel, owner), out_shape=jax.Shap...  28.7 us

profile of v8, /device:TPU:417, one launch (start us, length us, event | category | flops | bytes accessed | tf_op | source)
XLA Modules:
  0.0 76.7 jit_solution(935827222305142876)
XLA Ops:
  1.3 0.7 gather_panel.1
  2.0 0.0 copy-start
  2.0 0.0 copy-start.1
  2.0 0.0 copy-start.2
  2.1 0.0 copy-start.3
  2.1 28.8 %conditional.1 = (bf16[3,2,96,512]{3,2,1,0:T(8,128)(2,1)S(1)}) conditional(s32[]{:T(128)} %bitcast.1, bf16[6,2,96,512]{3,2,1,0:T(8,128)(2,1)S(1)} %gather_panel.1, bf16[6,2,96,512]{3,2,1,0:T(8,128)(2,1)S(1)} %gather_panel.1, bf16[6,2,96,512]{3,2,1,0:T(8,128)(2,1)S(1)} %gather_panel.1, ...), branch_computations={%region_0.0_spmd, %region_1.0_spmd, %region_2.0_spmd, %region_3.0_... | conditional | bytes 8 | solution.py:560
  2.1 28.7 %spread_panel.28 = bf16[3,2,96,512]{3,2,1,0:T(8,128)(2,1)S(1)} custom-call(bf16[6,2,96,512]{3,2,1,0:T(8,128)(2,1)S(1)} %panel_ref.12), custom_call_target="tpu_custom_call" | custom-call | tf_op jit(solution)/shard_map/cond/branch_12_fun/spread_panel/pallas_call | solution.py:285
  30.9 0.0 copy-done
  30.9 0.0 copy-done.1
  30.9 0.0 copy-done.2
  30.9 0.0 copy-done.3
  30.9 44.5 %row_sums.1 = bf16[2,6,128,512]{3,2,1,0:T(8,128)(2,1)S(1)} custom-call(s32[3,6]{1,0:T(4,128)S(1)} %bitcast.7, s32[1]{0:T(128)S(6)} %copy.25.step_ref, bf16[6,3,96,512]{3,2,1,0:T(8,128)(2,1)} %left_hbm.1, bf16[6,3,96,512]{3,2,1,0:T(8,128)(2,1)} %right_hbm.1, bf16[6,128,512]{2,1,0:T(8,128)(2,1)S(1)} %copy-done, ...), custom_call_target="tpu_custom_call" | custom-call | tf_op jit(solution)/shard_map/row_sums/pallas_call | solution.py:527
  75.4 1.2 %slice_bitcast_fusion = (bf16[6,128,512]{2,1,0:T(8,128)(2,1)}, bf16[6,128,512]{2,1,0:T(8,128)(2,1)}) fusion(bf16[2,6,128,512]{3,2,1,0:T(8,128)(2,1)S(1)} %row_sums.1), kind=kLoop, calls=%fused_computation | loop fusion | bytes 3145728 | tf_op jit(solution)/shard_map/squeeze | solution.py:564
Async XLA Ops:
  2.0 28.8 %copy-start = (bf16[6,128,512]{2,1,0:T(8,128)(2,1)S(1)}, bf16[6,128,512]{2,1,0:T(8,128)(2,1)}, u32[]{:S(2)}) copy-start(bf16[6,128,512]{2,1,0:T(8,128)(2,1)} %probe_hbm.1) | copy-start | bytes 2359300
  2.0 28.8 %copy-start.1 = (bf16[512,512]{1,0:T(8,128)(2,1)S(1)}, bf16[512,512]{1,0:T(8,128)(2,1)}, u32[]{:S(2)}) copy-start(bf16[512,512]{1,0:T(8,128)(2,1)} %solve_ref.1) | copy-start | bytes 1572868
  2.0 28.8 %copy-start.2 = (bf16[512,128]{1,0:T(8,128)(2,1)S(1)}, bf16[512,128]{1,0:T(8,128)(2,1)}, u32[]{:S(2)}) copy-start(bf16[512,128]{1,0:T(8,128)(2,1)} %sketch_ref.1) | copy-start | bytes 393220
  2.1 28.8 %copy-start.3 = (s32[6,3]{0,1:T(4,128)S(1)}, s32[6,3]{0,1:T(4,128)}, u32[]{:S(2)}) copy-start(s32[6,3]{0,1:T(4,128)} %param.25) | copy-start | bytes 220

commit v9 on v8

--- a/solution.py
+++ b/solution.py
@@ -397,12 +397,9 @@
             copy.wait()
         level = lax.broadcasted_iota(jnp.int32, (128, 96), 1)
         tiles = [c * 3 + j for j in range(3)]
-        both = [
-            dot_nt(right_ref[members(g), j].reshape(GROUP * 96, 512), upper_ref[j, 0]) for j in range(3)
-        ]
-        for k in range(GROUP):
+
+        def one_row(k, _):
             a = g * GROUP + k
-            part = slice(96 * k, 96 * (k + 1))
             live = z * 6 + a > column
             own_right = jnp.where(
                 tiles[0] == column,
@@ -417,7 +414,7 @@
                 depth = jnp.where(live & (tiles[j] <= column), ranks_ref[j, a], 0)
                 keep = level < depth
                 left = left_ref[a, j]
-                coupled = both[j][part].astype(BF16)
+                coupled = dot_nt(right_ref[a, j], upper_ref[j, 0]).astype(BF16)
                 mixed = jnp.where(own, own_mixed, dot_nt(reduced_ref[j], coupled))
                 mixed = jnp.where(keep, mixed, 0.0).astype(BF16)
                 probed = dot_nt(probe_ref[a], left)
@@ -429,6 +426,9 @@
                 co_sum += dot_nn(folded, closing)
             acc_ref[a] = -jnp.where(even, range_sum, co_sum)
             send_ref[a] = -jnp.where(even, co_sum, range_sum).astype(BF16)
+            return 0
+
+        lax.fori_loop(0, GROUP, one_row, 0)
 
         @pl.when(g == 0)
         def _():

time: 76.8 us -> 77.2 us (level)
  the two profiles are of different devices: /device:TPU:417 before, /device:TPU:481 now
where the time goes in v9:
time: 77.2 us; the launch traced here: 77 us
  Pallas kernels  74.3 us (96%)
  between operations  1.37 us (2%)
  local copies, waits for them, and re-layouts  1.27 us (2%)
    pallas_call x1, Pallas kernels, row_sums(): pl.pallas_call(row_kernel, out_shape=jax.ShapeDtypeStruct((2, 6, 128, 512...  47.2 us
    pallas_call x1, Pallas kernels, spread_panel(): pl.pallas_call(functools.partial(panel_kernel, owner), out_shape=jax.Shap...  26.3 us

profile of v9, /device:TPU:481, one launch (start us, length us, event | category | flops | bytes accessed | tf_op | source)
XLA Modules:
  0.0 77.0 jit_solution(5128332187598003046)
XLA Ops:
  1.3 0.7 gather_panel.1
  2.0 0.0 copy-start
  2.0 0.0 copy-start.1
  2.0 0.0 copy-start.2
  2.1 0.0 copy-start.3
  2.1 26.4 %conditional.1 = (bf16[3,2,96,512]{3,2,1,0:T(8,128)(2,1)S(1)}) conditional(s32[]{:T(128)} %bitcast.1, bf16[6,2,96,512]{3,2,1,0:T(8,128)(2,1)S(1)} %gather_panel.1, bf16[6,2,96,512]{3,2,1,0:T(8,128)(2,1)S(1)} %gather_panel.1, bf16[6,2,96,512]{3,2,1,0:T(8,128)(2,1)S(1)} %gather_panel.1, ...), branch_computations={%region_0.0_spmd, %region_1.0_spmd, %region_2.0_spmd, %region_3.0_... | conditional | bytes 8 | solution.py:560
  2.1 26.3 %spread_panel.21 = bf16[3,2,96,512]{3,2,1,0:T(8,128)(2,1)S(1)} custom-call(bf16[6,2,96,512]{3,2,1,0:T(8,128)(2,1)S(1)} %panel_ref.5), custom_call_target="tpu_custom_call" | custom-call | tf_op jit(solution)/shard_map/cond/branch_5_fun/spread_panel/pallas_call | solution.py:285
  28.5 0.0 copy-done
  28.5 0.0 copy-done.1
  28.5 0.0 copy-done.2
  28.5 0.0 copy-done.3
  28.5 47.2 %row_sums.1 = bf16[2,6,128,512]{3,2,1,0:T(8,128)(2,1)S(1)} custom-call(s32[3,6]{1,0:T(4,128)S(1)} %bitcast.7, s32[1]{0:T(128)S(6)} %copy.25.step_ref, bf16[6,3,96,512]{3,2,1,0:T(8,128)(2,1)} %left_hbm.1, bf16[6,3,96,512]{3,2,1,0:T(8,128)(2,1)} %right_hbm.1, bf16[6,128,512]{2,1,0:T(8,128)(2,1)S(1)} %copy-done, ...), custom_call_target="tpu_custom_call" | custom-call | tf_op jit(solution)/shard_map/row_sums/pallas_call | solution.py:527
  75.7 1.2 %slice_bitcast_fusion = (bf16[6,128,512]{2,1,0:T(8,128)(2,1)}, bf16[6,128,512]{2,1,0:T(8,128)(2,1)}) fusion(bf16[2,6,128,512]{3,2,1,0:T(8,128)(2,1)S(1)} %row_sums.1), kind=kLoop, calls=%fused_computation | loop fusion | bytes 3145728 | tf_op jit(solution)/shard_map/squeeze | solution.py:564
Async XLA Ops:
  2.0 26.4 %copy-start = (bf16[6,128,512]{2,1,0:T(8,128)(2,1)S(1)}, bf16[6,128,512]{2,1,0:T(8,128)(2,1)}, u32[]{:S(2)}) copy-start(bf16[6,128,512]{2,1,0:T(8,128)(2,1)} %probe_hbm.1) | copy-start | bytes 2359300
  2.0 26.4 %copy-start.1 = (bf16[512,512]{1,0:T(8,128)(2,1)S(1)}, bf16[512,512]{1,0:T(8,128)(2,1)}, u32[]{:S(2)}) copy-start(bf16[512,512]{1,0:T(8,128)(2,1)} %solve_ref.1) | copy-start | bytes 1572868
  2.0 26.4 %copy-start.2 = (bf16[512,128]{1,0:T(8,128)(2,1)S(1)}, bf16[512,128]{1,0:T(8,128)(2,1)}, u32[]{:S(2)}) copy-start(bf16[512,128]{1,0:T(8,128)(2,1)} %sketch_ref.1) | copy-start | bytes 393220
  2.1 26.4 %copy-start.3 = (s32[6,3]{0,1:T(4,128)S(1)}, s32[6,3]{0,1:T(4,128)}, u32[]{:S(2)}) copy-start(s32[6,3]{0,1:T(4,128)} %param.25) | copy-start | bytes 220
